TPU v7x, 256 devices: a whole 4x4x8 slice. The times are simulated.
256 devices in a mesh: dp: 64 (over y_lo, z, x), mp: 4 (over y_hi, core).
Axes of the slice: x: 4, y: 4 (y_hi: 2, y_lo: 2; y = y_hi * 2 + y_lo), z: 8, core: 2. Of those that a mesh axis runs over, the one named last changes fastest.
Arguments:
- activations: bfloat16 [4, 128, 256, 2048], P(None, 'dp', None, 'mp'), may hold values from -6 to 6
- out_grads: bfloat16 [4, 128, 256, 8192], P(None, 'dp', None, 'mp'), may hold values from -6 to 6
- proj_in: bfloat16 [4, 64, 2048], P(None, None, 'mp'), may hold values from -0.125 to 0.125
- proj_out: bfloat16 [4, 64, 8192], P(None, None, 'mp'), may hold values from -0.0625 to 0.0625
- query_grads: float32 [4, 64, 64, 64], P(None, 'dp'), may hold values from -6 to 6
Outputs:
- scores: float32 [128, 64], P('dp')
All inputs are finite; a program needn't handle non-finite values.
Results may differ from a plain program's by a relative error of at most 0.0003.
Values sent between devices are 32-bit elements; how exact they have to be, the bound alone decides.
No kernel may reach another device: no remote copies, remote signals or barrier semaphores. Data moves between devices by JAX's collectives and lax.ppermute only.
A program may use at most 128 MiB of HBM per device.

v0:
```python
import jax
import jax.numpy as jnp
from jax import lax
from jax.sharding import PartitionSpec as P

DAMP = 0.1


def precondition(fac_in, fac_out, queries):
    width = fac_in.shape[0]
    eye = jnp.eye(width, dtype=jnp.float32)
    damped_in = fac_in + DAMP * jnp.trace(fac_in) / width * eye
    damped_out = fac_out + DAMP * jnp.trace(fac_out) / width * eye
    chol_in = jnp.linalg.cholesky(damped_in)
    chol_out = jnp.linalg.cholesky(damped_out)
    left = jax.vmap(lambda block: jax.scipy.linalg.cho_solve((chol_in, True), block))(queries)
    return jax.vmap(lambda block: jax.scipy.linalg.cho_solve((chol_out, True), block.T).T)(left)


def fetch_queries(queries):
    return lax.all_gather(queries, "dp", axis=1, tiled=True)


def project(inputs, factor):
    return lax.dot_general(
        inputs, factor, (((1,), (1,)), ((), ())), preferred_element_type=jnp.float32
    )


def local(activations, out_grads, proj_in, proj_out, query_grads):
    layers = activations.shape[0]
    clip_dev = activations.shape[1]
    frames = activations.shape[2]
    rank = proj_in.shape[1]
    rows = clip_dev * frames
    root = jnp.sqrt(jnp.float32(frames))
    high = lax.Precision.HIGHEST
    gathered = fetch_queries(query_grads)
    fac_list_in = []
    fac_list_out = []
    grad_list = []
    for layer in range(layers):
        flat_x = activations[layer].reshape(rows, activations.shape[3])
        flat_g = out_grads[layer].reshape(rows, out_grads.shape[3])
        partial_proj = jnp.concatenate(
            [project(flat_x, proj_in[layer]), project(flat_g, proj_out[layer])], axis=1
        )
        summed = lax.psum(partial_proj, "mp")
        xp = summed[:, :rank]
        gp = summed[:, rank:]
        clip_grads = (
            jnp.einsum(
                "cfi,cfj->cij",
                xp.reshape(clip_dev, frames, rank),
                gp.reshape(clip_dev, frames, rank),
                precision=high,
            )
            / root
        )
        fac_list_in.append(jnp.dot(xp.T, xp, precision=high))
        fac_list_out.append(jnp.dot(gp.T, gp, precision=high))
        grad_list.append(clip_grads)
    stacked_in = jnp.stack(fac_list_in)
    stacked_out = jnp.stack(fac_list_out)
    total = jnp.float32(rows * lax.axis_size("dp"))
    sum_in, sum_out = lax.psum((stacked_in, stacked_out), "dp")
    sum_in = sum_in / total
    sum_out = sum_out / total
    conditioned = jnp.stack(
        [precondition(sum_in[layer], sum_out[layer], gathered[layer]) for layer in range(layers)]
    )
    grads_all = jnp.stack(grad_list)
    scores = jnp.einsum("lcij,lqij->cq", grads_all, conditioned, precision=high)
    return scores / jnp.sqrt(jnp.float32(layers * rank * rank))


def solution(mesh):
    placed = (
        P(None, "dp", None, "mp"),
        P(None, "dp", None, "mp"),
        P(None, None, "mp"),
        P(None, None, "mp"),
        P(None, "dp", None, None),
    )
    return jax.shard_map(
        local, mesh=mesh, in_specs=placed, out_specs=P("dp", None), check_vma=False
    )
```

profile of v0, /device:TPU:24, one launch (start us, length us, event | category | flops | bytes accessed | tf_op | source)
XLA Modules:
  0.0 1085.2 jit_solution(15109579514485189336)
XLA Ops:
  6.5 1.7 fusion.94
  9.4 4.1 fusion.93
  19.5 52.1 %all-reduce.7.cloned.1.call-done = (f32[512,128]{0,1:T(8,128)}, f32[512,128]{0,1:T(8,128)}, f32[512,128]{0,1:T(8,128)}, f32[512,128]{0,1:T(8,128)}) async-done(((f32[512,128]{0,1:T(8,128)}, f32[512,128]{0,1:T(8,128)}, f32[512,128]{0,1:T(8,128)}, f32[512,128]{0,1:T(8,128)}), (f32[512,128]{0,1:T(8,128)}, f32[512,128]{0,1:T(8,128)}, f32[512,128]{0,1:T(8,128)}, ...) | async-done | bytes 1048592 | tf_op jit(solution)/shard_map/psum | solution.py:48
  71.6 1.3 convolution_bitcast_fusion.20
  72.9 1.2 convolution_bitcast_fusion.16
  74.1 1.2 convolution_bitcast_fusion.21
  75.4 1.2 convolution_bitcast_fusion.17
  76.6 1.2 convolution_bitcast_fusion.22
  77.9 1.2 convolution_bitcast_fusion.18
  79.1 1.3 convolution_bitcast_fusion.23
  80.4 1.2 convolution_bitcast_fusion.19
  85.0 550.6 %all-reduce.5.cloned.1.call-done = (f32[4,64,64]{1,2,0:T(8,128)}, f32[4,64,64]{1,2,0:T(8,128)}) async-done(((f32[4,64,64]{1,2,0:T(8,128)}, f32[4,64,64]{1,2,0:T(8,128)}), (f32[4,64,64]{1,2,0:T(8,128)}, f32[4,64,64]{1,2,0:T(8,128)})) %all-reduce.5.cloned.1.call-update) | async-done | bytes 131088 | tf_op jit(solution)/shard_map/psum | solution.py:66
  642.7 5.8 cholesky.134
  649.9 4.9 custom-call.15
  654.9 5.8 cholesky.200
  662.1 4.9 custom-call.21
  667.1 5.8 cholesky.178
  674.3 4.9 custom-call.19
  679.3 5.8 cholesky.156
  686.5 5.5 custom-call.17
  692.1 5.8 cholesky.145
  699.3 4.9 custom-call.14
  704.3 5.8 cholesky.211
  711.5 5.5 custom-call.20
  717.3 5.8 cholesky.189
  724.5 5.5 custom-call.18
  730.1 5.9 cholesky.167
  737.3 5.5 custom-call.16
  742.8 206.5 %all-gather.2.cloned.1.call-done = f32[4,64,64,64]{3,2,1,0:T(8,128)} async-done(((f32[4,1,64,64]{3,2,1,0:T(8,128)}), f32[4,64,64,64]{3,2,1,0:T(8,128)}) %all-gather.2.cloned.1.call-update) | async-done | bytes 4194320 | tf_op jit(solution)/shard_map/all_gather | solution.py:21
  949.3 7.5 slice_bitcast_fusion.3
  956.8 2.4 copy.58
  959.8 2.4 copy.73
  962.2 1.6 reshape.60
  963.8 2.4 copy.68
  966.2 1.6 reshape.58
  967.9 2.4 copy.63
  970.2 1.6 reshape.56
  971.9 3.3 convolution_bitcast_fusion.5
  975.1 1.8 copy.90
  976.9 8.2 convolution_bitcast_fusion.13
  985.1 2.3 reshape.57
  987.5 2.0 convolution_bitcast_fusion.4
  989.5 1.8 copy.91
  991.4 8.3 convolution_bitcast_fusion.12
  999.7 2.0 convolution_bitcast_fusion.3
  1001.7 1.8 copy.92
  1003.5 8.1 convolution_bitcast_fusion.11
  1011.6 2.5 reshape.59
  1014.2 2.0 convolution_bitcast_fusion.2
  1016.2 1.8 copy.93
  1018.1 7.4 convolution_bitcast_fusion.10
  1025.4 2.0 convolution_bitcast_fusion.1
  1027.4 1.8 copy.94
  1029.3 7.4 convolution_bitcast_fusion.9
  1036.7 2.3 reshape.61
  1039.0 2.0 convolution_bitcast_fusion
  1041.0 1.8 copy.95
  1042.8 7.4 convolution_bitcast_fusion.8
  1050.2 2.0 convolution_bitcast_fusion.7
  1052.3 1.8 copy.88
  1054.1 7.4 convolution_bitcast_fusion.15
  1061.5 2.3 reshape.55
  1065.5 6.1 convolution_bitcast_fusion.14
  1071.6 6.8 fusion.9
  (103 shorter events, 26.3 us)
Async XLA Ops:
  6.5 65.0 %all-reduce.7.cloned.1.call-start = ((), (), s32[]{:S(2)}) async-start(), calls=%async_computation.2 | async-start | bytes 2097152 | tf_op jit(solution)/shard_map/psum | solution.py:48
  6.5 1.7 copy-start.9
  9.4 4.1 copy-start.4
  19.5 616.1 %all-reduce.5.cloned.1.call-start = ((), (), s32[]{:S(2)}) async-start(), calls=%async_computation.1 | async-start | bytes 524288 | tf_op jit(solution)/shard_map/psum | solution.py:66
  71.6 12.2 %copy-start.7 = (f32[512,128]{0,1:T(8,128)S(1)}, f32[512,128]{0,1:T(8,128)}, u32[]{:S(2)}) copy-start(f32[512,128]{0,1:T(8,128)} %get-tuple-element.17) | copy-start | bytes 786436
  71.6 12.2 %copy-start.8 = (f32[512,128]{0,1:T(8,128)S(1)}, f32[512,128]{0,1:T(8,128)}, u32[]{:S(2)}) copy-start(f32[512,128]{0,1:T(8,128)} %get-tuple-element.18) | copy-start | bytes 786436
  71.6 12.5 %copy-start.5 = (f32[512,128]{0,1:T(8,128)S(1)}, f32[512,128]{0,1:T(8,128)}, u32[]{:S(2)}) copy-start(f32[512,128]{0,1:T(8,128)} %get-tuple-element.19) | copy-start | bytes 786436
  71.6 12.5 %copy-start.6 = (f32[512,128]{0,1:T(8,128)S(1)}, f32[512,128]{0,1:T(8,128)}, u32[]{:S(2)}) copy-start(f32[512,128]{0,1:T(8,128)} %get-tuple-element.20) | copy-start | bytes 786436
  83.0 866.3 %all-gather.2.cloned.1.call-start = ((), (), s32[]{:S(2)}) async-start(), calls=%async_computation | async-start | bytes 8519680 | tf_op jit(solution)/shard_map/all_gather | solution.py:21
  985.1 2.4 copy-start.10
  991.4 8.3 copy-start.1
  991.4 8.3 copy-start.13
  1018.0 7.4 copy-start
  1018.0 7.4 copy-start.11
  1027.4 1.8 copy-start.12
  1065.5 6.1 copy-start.2
  1065.5 6.1 copy-start.3
Sparse Core Ops, SparseCore 0:
  19.6 51.9 all-reduce.6
  83.1 552.3 all-reduce.4
  637.3 311.9 all-gather.1
where the time goes:
time: 1090 us
  waiting for transfers between devices  809 us (74%)
  other arithmetic  106 us (10%)
  matrix products  98.7 us (9%)
  local copies, waits for them, and re-layouts  51.9 us (5%)
  between operations  19 us (2%)
    psum x1, waiting for transfers between devices, local(): sum_in, sum_out = lax.psum((stacked_in, stacked_out), 'dp')  551 us
    all_gather x1, waiting for transfers between devices, fetch_queries(): return lax.all_gather(queries, 'dp', axis=1, tiled=True)  207 us
    psum x1, waiting for transfers between devices, local(): summed = lax.psum(partial_proj, 'mp')  52.1 us
    another operation x8, matrix products, precondition(): jax.scipy.linalg.cho_solve((chol_in, True), block)  40.5 us
    another operation x8, matrix products, precondition(): jax.scipy.linalg.cho_solve((chol_out, True), block.T)  36.2 us
    another operation x12, other arithmetic, precondition(): chol_in = jnp.linalg.cholesky(damped_in)  26.1 us
    another operation x12, other arithmetic, precondition(): chol_out = jnp.linalg.cholesky(damped_out)  26.1 us
    another operation x8, other arithmetic, precondition(): jax.scipy.linalg.cho_solve((chol_in, True), block)  24.1 us
  transfers between devices with their start and end apart: 3, of which 3 were waited for; matrix products, arithmetic and copies ran while one was open for 10% of the time, Pallas kernels for 0%

commit v1 on v0

v1 whole, which is shorter than its diff:
```python
import functools

import jax
import jax.numpy as jnp
from jax import lax
from jax.experimental import pallas as pl
from jax.experimental.pallas import tpu as pltpu
from jax.sharding import PartitionSpec as P

DAMP = 0.1
QUERY_VMEM = 56426496
VMEM = 53 * 2**20 + 2**19
QUERY_BITS = (8, 24, 4, 32, 1, 3)
QUERY_AT = {1: 3, 2: 4, 4: 5}
FACTOR_BITS = (1, 3, 4, 8, 24, 32)
HIGH = lax.Precision.HIGHEST


def xor_pairs(size, bit):
    return [(i, i ^ bit) for i in range(size)]


def project_kernel(offset, has_query, x_hbm, g_hbm, pi_hbm, po_hbm, *rest):
    if has_query:
        query_hbm, out, own, xs, gs, pis, pos, sems, block, query_sem = rest
    else:
        out, xs, gs, pis, pos, sems = rest
    rows, wide = out.shape
    rank = wide // 2
    me = lax.axis_index("mp")
    layer = me ^ offset
    copies = [
        pltpu.make_async_copy(source.at[layer], target, sems.at[index])
        for index, (source, target) in enumerate(
            ((pi_hbm, pis), (x_hbm, xs), (po_hbm, pos), (g_hbm, gs))
        )
    ]
    if has_query:
        fetch = pltpu.make_async_copy(query_hbm.at[me, 0], block, query_sem)
        fetch.start()
    for copy in copies:
        copy.start()
    for copy in copies:
        copy.wait()
    contract = (((1,), (1,)), ((), ()))
    out[:, :rank] = lax.dot_general(
        xs[...].reshape(rows, xs.shape[2]), pis[...], contract, preferred_element_type=jnp.float32
    )
    out[:, rank:] = lax.dot_general(
        gs[...].reshape(rows, gs.shape[2]), pos[...], contract, preferred_element_type=jnp.float32
    )
    if has_query:
        fetch.wait()
        own[0, :, :rank] = block[: rank // 2]
        own[0, :, rank:] = block[rank // 2 :]


def project(offset, args, query=None, after=None):
    activations, out_grads, proj_in, proj_out = args
    if after is not None:
        proj_in, _ = lax.optimization_barrier((proj_in, after))
    _, clips, frames, width = activations.shape
    hidden = out_grads.shape[3]
    rank = proj_in.shape[1]
    rows = clips * frames
    kind = activations.dtype
    anywhere = pl.BlockSpec(memory_space=pl.ANY)
    vmem = pl.BlockSpec(memory_space=pltpu.VMEM)
    out_shape = jax.ShapeDtypeStruct((rows, 2 * rank), jnp.float32)
    scratch = [
        pltpu.VMEM((clips, frames, width), kind),
        pltpu.VMEM((clips, frames, hidden), kind),
        pltpu.VMEM((rank, width), kind),
        pltpu.VMEM((rank, hidden), kind),
        pltpu.SemaphoreType.DMA((4,)),
    ]
    operands, out_specs = [activations, out_grads, proj_in, proj_out], vmem
    if query is not None:
        operands.append(query)
        out_specs = [vmem, vmem]
        out_shape = [out_shape, jax.ShapeDtypeStruct((1, rank // 2, 2 * rank), jnp.float32)]
        scratch += [pltpu.VMEM((rank, rank), jnp.float32), pltpu.SemaphoreType.DMA]
    return pl.pallas_call(
        functools.partial(project_kernel, offset, query is not None),
        in_specs=[anywhere] * len(operands),
        out_specs=out_specs,
        out_shape=out_shape,
        scratch_shapes=scratch,
        compiler_params=pltpu.CompilerParams(vmem_limit_bytes=VMEM if query is None else QUERY_VMEM),
        cost_estimate=pl.CostEstimate(
            flops=rows * (width + hidden) * rank * 2,
            bytes_accessed=rows * (width + hidden) * 2 + rows * rank * 8,
            transcendentals=0,
        ),
        name="project",
    )(*operands)


def moments_kernel(clips, a_ref, b_ref, fac_ref, grad_ref):
    z = a_ref[...] + b_ref[...]
    rows, wide = z.shape
    rank = wide // 2
    frames = rows // clips
    total = None
    for clip in range(clips):
        part = z[clip * frames : (clip + 1) * frames]
        moment = lax.dot_general(
            part, part, (((0,), (0,)), ((), ())), precision=HIGH, preferred_element_type=jnp.float32
        )
        total = moment if total is None else total + moment
        grad_ref[:, clip * rank : (clip + 1) * rank] = moment[:rank, rank:]
    fac_ref[:, :rank] = total[:rank, :rank]
    fac_ref[:, rank:] = total[rank:, rank:]


def moments(clips, a, b):
    rows, wide = a.shape
    rank = wide // 2
    return pl.pallas_call(
        functools.partial(moments_kernel, clips),
        out_shape=[
            jax.ShapeDtypeStruct((rank, wide), jnp.float32),
            jax.ShapeDtypeStruct((rank, clips * rank), jnp.float32),
        ],
        compiler_params=pltpu.CompilerParams(vmem_limit_bytes=8 * 2**20),
        name="moments",
    )(a, b)


def solve_kernel(clips, total, fa_ref, fb_ref, grad_ref, out_ref):
    rank, wide = fa_ref.shape
    half = rank // 2
    fac = (fa_ref[...] + fb_ref[...]) * (1.0 / total)
    row = lax.broadcasted_iota(jnp.int32, (rank, wide), 0)
    lane = lax.broadcasted_iota(jnp.int32, (rank, wide), 1)
    left = lane < rank
    eye = (row == lane) | (row + rank == lane)
    diag = jnp.where(eye, fac, 0.0)
    trace_l = jnp.sum(jnp.where(left, diag, 0.0))
    trace_r = jnp.sum(jnp.where(left, 0.0, diag))
    damp = jnp.where(left, trace_l, trace_r) * (DAMP / rank)
    mat = fac + jnp.where(eye, damp, 0.0)
    def column(source, k):
        return jnp.where(left, source[:, k : k + 1], source[:, rank + k : rank + k + 1])

    c0, c1 = column(mat, 0), column(mat, 1)
    for k in range(0, rank, 2):
        ahead = [column(mat, j) for j in (k + 2, k + 3) if j < rank]
        a, b, d = c0[k : k + 1], c0[k + 1 : k + 2], c1[k + 1 : k + 2]
        at0 = (lane == k) | (lane == rank + k)
        at1 = (lane == k + 1) | (lane == rank + k + 1)
        scale = 1.0 / (a * d - b * b)
        a, b, d = a * scale, b * scale, d * scale
        r0 = jnp.where(at0[:1], 1.0, jnp.where(at1[:1], 0.0, mat[k : k + 1]))
        r1 = jnp.where(at1[:1], 1.0, jnp.where(at0[:1], 0.0, mat[k + 1 : k + 2]))
        n0 = d * r0 - b * r1
        n1 = a * r1 - b * r0
        rest = jnp.where(at0 | at1, 0.0, mat) - c0 * n0 - c1 * n1
        mat = jnp.where(row == k, n0, jnp.where(row == k + 1, n1, rest))
        following = []
        for col in ahead:
            u, v = col[k : k + 1], col[k + 1 : k + 2]
            m0 = d * u - b * v
            m1 = a * v - b * u
            rest = col - c0 * m0 - c1 * m1
            following.append(jnp.where(row == k, m0, jnp.where(row == k + 1, m1, rest)))
        if following:
            c0, c1 = following
    inv_in = mat[:, :rank]
    inv_out = mat[:, rank:]
    left_solved = jnp.dot(inv_in, grad_ref[...], precision=HIGH, preferred_element_type=jnp.float32)
    for clip in range(clips):
        solved = jnp.dot(
            left_solved[:, clip * rank : (clip + 1) * rank], inv_out, precision=HIGH,
            preferred_element_type=jnp.float32,
        )
        out_ref[clip, :, :rank] = solved[:half]
        out_ref[clip, :, rank:] = solved[half:]


def solve(clips, total, fa, fb, grads):
    rank, wide = fa.shape
    vmem = pl.BlockSpec(memory_space=pltpu.VMEM)
    return pl.pallas_call(
        functools.partial(solve_kernel, clips, total),
        in_specs=[vmem] * 3,
        out_specs=vmem,
        out_shape=jax.ShapeDtypeStruct((clips, rank // 2, wide), jnp.float32),
        compiler_params=pltpu.CompilerParams(vmem_limit_bytes=8 * 2**20),
        cost_estimate=pl.CostEstimate(flops=0, bytes_accessed=8_000_000, transcendentals=0),
        name="solve",
    )(fa, fb, grads)


def contract_kernel(scale, solved_ref, q_ref, out_ref):
    at = lax.axis_index("dp").astype(jnp.int32)
    queries, half, wide = q_ref.shape
    clips = solved_ref.shape[0]
    q_at = lax.broadcasted_iota(jnp.int32, (queries, queries * 8), 0)
    r_at = lax.broadcasted_iota(jnp.int32, (queries, queries * 8), 1) // 8
    came = at
    for index, bit in enumerate(QUERY_BITS):
        came = came ^ jnp.where((r_at >> index) & 1 == 1, bit, 0)
    select = jnp.where(came == q_at, 1.0, 0.0)
    q = q_ref[...].reshape(queries, half // 8, 8, wide)
    partial = jnp.concatenate(
        [
            jnp.sum(q * solved_ref[clip].reshape(1, half // 8, 8, wide), axis=1).reshape(
                queries * 8, wide
            )
            for clip in range(clips)
        ],
        axis=1,
    )
    per_query = jnp.dot(select, partial, precision=HIGH, preferred_element_type=jnp.float32)
    ones = jnp.full((8, wide), scale, jnp.float32)
    for clip in range(clips):
        line = lax.dot_general(
            ones, per_query[:, clip * wide : (clip + 1) * wide], (((1,), (1,)), ((), ())),
            precision=HIGH, preferred_element_type=jnp.float32,
        )
        out_ref[clip : clip + 1, :] = line[:1]


def contract(scale, solved, queries):
    vmem = pl.BlockSpec(memory_space=pltpu.VMEM)
    return pl.pallas_call(
        functools.partial(contract_kernel, scale),
        in_specs=[vmem] * 2,
        out_specs=vmem,
        out_shape=jax.ShapeDtypeStruct((solved.shape[0], queries.shape[0]), jnp.float32),
        compiler_params=pltpu.CompilerParams(vmem_limit_bytes=16 * 2**20),
        name="contract",
    )(solved, queries)


def local(activations, out_grads, proj_in, proj_out, query_grads):
    layers, clips, frames, _ = activations.shape
    rank = proj_in.shape[1]
    members = lax.axis_size("mp")
    groups = lax.axis_size("dp")
    me = lax.axis_index("mp")

    def widen(blocks, index, after):
        blocks, _ = lax.optimization_barrier((blocks, after))
        pairs = xor_pairs(groups, QUERY_BITS[index])
        return jnp.concatenate([blocks, lax.ppermute(blocks, "dp", pairs)])

    args = (activations, out_grads, proj_in, proj_out)
    far, gathered = project(3, args, query=query_grads)
    far_in = lax.ppermute(far, "mp", xor_pairs(members, 1))
    cross = project(2, args, after=far) + far_in
    cross_in = lax.ppermute(cross, "mp", xor_pairs(members, 2))
    near = project(1, args, after=cross)
    near_in = lax.ppermute(near, "mp", xor_pairs(members, 1))
    mine = project(0, args, after=near)
    gathered = widen(gathered, 0, far)
    gathered = widen(gathered, 1, near)
    gathered = widen(gathered, 2, mine)
    fac, grads = moments(clips, mine + cross_in, near_in)
    for step, bit in enumerate(FACTOR_BITS[:-1]):
        if step in QUERY_AT:
            gathered = widen(gathered, QUERY_AT[step], fac)
        fac = fac + lax.ppermute(fac, "dp", xor_pairs(groups, bit))
    other = lax.ppermute(fac, "dp", xor_pairs(groups, FACTOR_BITS[-1]))
    solved = solve(clips, clips * frames * groups, fac, other, grads)
    scale = 1.0 / (frames**0.5 * (layers * rank * rank) ** 0.5)
    out = contract(scale, solved, gathered)
    out = out + lax.ppermute(out, "mp", xor_pairs(members, 1))
    return out + lax.ppermute(out, "mp", xor_pairs(members, 2))


def solution(mesh):
    placed = (
        P(None, "dp", None, "mp"),
        P(None, "dp", None, "mp"),
        P(None, None, "mp"),
        P(None, None, "mp"),
        P(None, "dp", None, None),
    )
    return jax.shard_map(
        local, mesh=mesh, in_specs=placed, out_specs=P("dp", None), check_vma=False
    )
```

time: 1090 us -> 68.2 us (0.06)
  the two profiles are of different devices: /device:TPU:24 before, /device:TPU:1 now
where the time goes in v1:
time: 68.2 us; the launch traced here: 68 us
  starting transfers between devices  35.8 us (52%)
  Pallas kernels  16 us (23%)
  waiting for transfers between devices  15.3 us (22%)
  other arithmetic  0.8 us (1%)
    pallas_call x4, Pallas kernels, project(): pl.pallas_call(functools.partial(project_kernel, offset, query is not Non...  11.9 us
    ppermute x5, waiting for transfers between devices, local(): fac = fac + lax.ppermute(fac, 'dp', xor_pairs(groups, bit))  10.2 us
    ppermute x6, starting transfers between devices, widen(): return jnp.concatenate([blocks, lax.ppermute(blocks, 'dp', pairs)])  9.45 us
    ppermute x1, starting transfers between devices, local(): out = out + lax.ppermute(out, 'mp', xor_pairs(members, 1))  8.57 us
    ppermute x5, starting transfers between devices, local(): fac = fac + lax.ppermute(fac, 'dp', xor_pairs(groups, bit))  7.66 us
    ppermute x1, starting transfers between devices, local(): far_in = lax.ppermute(far, 'mp', xor_pairs(members, 1))  3.33 us
    ppermute x1, starting transfers between devices, local(): cross_in = lax.ppermute(cross, 'mp', xor_pairs(members, 2))  3 us
    pallas_call x1, Pallas kernels, solve(): pl.pallas_call(functools.partial(solve_kernel, clips, total), in_specs=[v...  2.81 us
  transfers between devices with their start and end apart: 17, of which 9 were waited for; matrix products, arithmetic and copies ran while one was open for 0% of the time, Pallas kernels for 17%

profile of v1, /device:TPU:1, one launch (start us, length us, event | category | flops | bytes accessed | tf_op | source)
XLA Modules:
  0.0 68.0 jit_solution(17108127369260702497)
XLA Ops:
  0.0 3.5 %project.4 = (f32[512,128]{1,0:T(8,128)}, f32[1,32,128]{2,1,0:T(8,128)S(1)}) custom-call(bf16[4,2,256,512]{3,2,1,0:T(8,128)(2,1)} %x_hbm.7, bf16[4,2,256,2048]{3,2,1,0:T(8,128)(2,1)} %g_hbm.7, bf16[4,64,512]{2,1,0:T(8,128)(2,1)} %pi_hbm.4, bf16[4,64,2048]{2,1,0:T(8,128)(2,1)} %po_hbm.7, f32[4,1,64,64]{3,2,1,0:T(8,128)} %rest_0_.1), custom_call_target="tpu_custom_call" | custom-call | flops 167772160 | bytes 2883584 | tf_op jit(solution)/shard_map/project/pallas_call | solution.py:83
  3.5 3.3 %collective-permute-start = (f32[512,128]{1,0:T(8,128)}, f32[512,128]{1,0:T(8,128)S(1)}, u32[]{:S(2)}, u32[]{:S(2)}) collective-permute-start(f32[512,128]{1,0:T(8,128)} %get-tuple-element.18), channel_id=1, source_target_pairs={{0,1},{1,0},{2,3},{3,2},{4,5},{5,4},{6,7},{7,6},{8,9},{9,8},{10,11... | collective-permute-start | bytes 786440 | tf_op jit(solution)/shard_map/ppermute | solution.py:251
  6.9 1.3 %collective-permute-start.9 = (f32[1,32,128]{2,1,0:T(8,128)S(1)}, f32[1,32,128]{2,1,0:T(8,128)S(1)}, u32[]{:S(2)}, u32[]{:S(2)}) collective-permute-start(f32[1,32,128]{2,1,0:T(8,128)S(1)} %get-tuple-element.25), channel_id=1, source_target_pairs={{0,32},{4,36},{8,40},{12,44},{16,48},{20,52},{24,56},{28,60},{32,0... | collective-permute-start | bytes 49160 | tf_op jit(solution)/shard_map/ppermute | solution.py:247
  8.1 2.8 %project.5 = f32[512,128]{1,0:T(8,128)S(1)} custom-call(bf16[4,2,256,512]{3,2,1,0:T(8,128)(2,1)} %x_hbm.7, bf16[4,2,256,2048]{3,2,1,0:T(8,128)(2,1)} %g_hbm.7, bf16[4,64,512]{2,1,0:T(8,128)(2,1)} %pi_hbm.4, bf16[4,64,2048]{2,1,0:T(8,128)(2,1)} %po_hbm.7), custom_call_target="tpu_custom_call" | custom-call | flops 167772160 | bytes 2883584 | tf_op jit(solution)/shard_map/project/pallas_call | solution.py:83
  11.0 0.0 collective-permute-done
  11.0 3.0 %collective-permute-start.1 = (f32[512,128]{1,0:T(8,128)S(1)}, f32[512,128]{1,0:T(8,128)S(1)}, u32[]{:S(2)}, u32[]{:S(2)}) collective-permute-start(f32[512,128]{1,0:T(8,128)S(1)} %add.27), channel_id=1, source_target_pairs={{0,2},{1,3},{2,0},{3,1},{4,6},{5,7},{6,4},{7,5},{8,10},{9,11},{10,... | collective-permute-start | bytes 786440 | tf_op jit(solution)/shard_map/ppermute | solution.py:253
  14.0 2.8 %project.6 = f32[512,128]{1,0:T(8,128)S(1)} custom-call(bf16[4,2,256,512]{3,2,1,0:T(8,128)(2,1)} %x_hbm.7, bf16[4,2,256,2048]{3,2,1,0:T(8,128)(2,1)} %g_hbm.7, bf16[4,64,512]{2,1,0:T(8,128)(2,1)} %pi_hbm.4, bf16[4,64,2048]{2,1,0:T(8,128)(2,1)} %po_hbm.7), custom_call_target="tpu_custom_call" | custom-call | flops 167772160 | bytes 2883584 | tf_op jit(solution)/shard_map/project/pallas_call | solution.py:83
  16.8 0.7 %collective-permute-start.2 = (f32[512,128]{1,0:T(8,128)S(1)}, f32[512,128]{1,0:T(8,128)S(1)}, u32[]{:S(2)}, u32[]{:S(2)}) collective-permute-start(f32[512,128]{1,0:T(8,128)S(1)} %project.6), channel_id=1, source_target_pairs={{0,1},{1,0},{2,3},{3,2},{4,5},{5,4},{6,7},{7,6},{8,9},{9,8},{10,11... | collective-permute-start | bytes 786440 | tf_op jit(solution)/shard_map/ppermute | solution.py:255
  17.5 0.0 collective-permute-done.9
  17.6 4.2 %collective-permute-start.10 = (f32[2,32,128]{2,1,0:T(8,128)S(1)}, f32[2,32,128]{2,1,0:T(8,128)S(1)}, u32[]{:S(2)}, u32[]{:S(2)}) collective-permute-start(f32[2,32,128]{2,1,0:T(8,128)S(1)} %pad_maximum_fusion.5), channel_id=1, source_target_pairs={{0,96},{4,100},{8,104},{12,108},{16,112},{20,116},{24,120},{28,124... | collective-permute-start | bytes 98312 | tf_op jit(solution)/shard_map/ppermute | solution.py:247
  21.8 2.8 %project.7 = f32[512,128]{1,0:T(8,128)S(1)} custom-call(bf16[4,2,256,512]{3,2,1,0:T(8,128)(2,1)} %x_hbm.7, bf16[4,2,256,2048]{3,2,1,0:T(8,128)(2,1)} %g_hbm.7, bf16[4,64,512]{2,1,0:T(8,128)(2,1)} %pi_hbm.4, bf16[4,64,2048]{2,1,0:T(8,128)(2,1)} %po_hbm.7), custom_call_target="tpu_custom_call" | custom-call | flops 167772160 | bytes 2883584 | tf_op jit(solution)/shard_map/project/pallas_call | solution.py:83
  24.6 0.0 collective-permute-done.10
  24.6 0.8 %collective-permute-start.11 = (f32[4,32,128]{2,1,0:T(8,128)S(1)}, f32[4,32,128]{2,1,0:T(8,128)S(1)}, u32[]{:S(2)}, u32[]{:S(2)}) collective-permute-start(f32[4,32,128]{2,1,0:T(8,128)S(1)} %pad_maximum_fusion.4), channel_id=1, source_target_pairs={{0,16},{4,20},{8,24},{12,28},{16,0},{20,4},{24,8},{28,12},{32,48},... | collective-permute-start | bytes 196616 | tf_op jit(solution)/shard_map/ppermute | solution.py:247
  25.4 0.0 collective-permute-done.1
  25.4 0.0 collective-permute-done.2.b_ref
  25.5 0.4 moments.1
  25.9 1.3 %collective-permute-start.3 = (f32[64,128]{1,0:T(8,128)S(1)}, f32[64,128]{1,0:T(8,128)S(1)}, u32[]{:S(2)}, u32[]{:S(2)}) collective-permute-start(f32[64,128]{1,0:T(8,128)S(1)} %get-tuple-element.22), channel_id=1, source_target_pairs={{0,4},{4,0},{8,12},{12,8},{16,20},{20,16},{24,28},{28,24},{32,36},... | collective-permute-start | bytes 98312 | tf_op jit(solution)/shard_map/ppermute | solution.py:264
  27.2 0.6 collective-permute-done.11
  27.8 1.2 %collective-permute-done.3 = f32[64,128]{1,0:T(8,128)S(1)} collective-permute-done((f32[64,128]{1,0:T(8,128)S(1)}, f32[64,128]{1,0:T(8,128)S(1)}, u32[]{:S(2)}, u32[]{:S(2)}) %collective-permute-start.3) | collective-permute-done | bytes 32800 | tf_op jit(solution)/shard_map/ppermute | solution.py:264
  29.0 0.4 collective-permute-start.12
  29.4 2.5 %collective-permute-start.4 = (f32[64,128]{1,0:T(8,128)S(1)}, f32[64,128]{1,0:T(8,128)S(1)}, u32[]{:S(2)}, u32[]{:S(2)}) collective-permute-start(f32[64,128]{1,0:T(8,128)S(1)} %add.29), channel_id=1, source_target_pairs={{0,12},{4,8},{8,4},{12,0},{16,28},{20,24},{24,20},{28,16},{32,44},... | collective-permute-start | bytes 98312 | tf_op jit(solution)/shard_map/ppermute | solution.py:264
  31.9 1.5 %collective-permute-done.4 = f32[64,128]{1,0:T(8,128)S(1)} collective-permute-done((f32[64,128]{1,0:T(8,128)S(1)}, f32[64,128]{1,0:T(8,128)S(1)}, u32[]{:S(2)}, u32[]{:S(2)}) %collective-permute-start.4) | collective-permute-done | bytes 32800 | tf_op jit(solution)/shard_map/ppermute | solution.py:264
  33.4 0.0 collective-permute-done.12
  33.4 0.7 %collective-permute-start.13 = (f32[16,32,128]{2,1,0:T(8,128)S(1)}, f32[16,32,128]{2,1,0:T(8,128)S(1)}, u32[]{:S(2)}, u32[]{:S(2)}) collective-permute-start(f32[16,32,128]{2,1,0:T(8,128)S(1)} %pad_maximum_fusion.2), channel_id=1, source_target_pairs={{0,4},{4,0},{8,12},{12,8},{16,20},{20,16},{24,28},{28,24},{32,36},... | collective-permute-start | bytes 786440 | tf_op jit(solution)/shard_map/ppermute | solution.py:247
  34.1 0.8 %collective-permute-start.5 = (f32[64,128]{1,0:T(8,128)S(1)}, f32[64,128]{1,0:T(8,128)S(1)}, u32[]{:S(2)}, u32[]{:S(2)}) collective-permute-start(f32[64,128]{1,0:T(8,128)S(1)} %add.30), channel_id=1, source_target_pairs={{0,16},{4,20},{8,24},{12,28},{16,0},{20,4},{24,8},{28,12},{32,48},... | collective-permute-start | bytes 98312 | tf_op jit(solution)/shard_map/ppermute | solution.py:264
  34.9 2.0 %collective-permute-done.5 = f32[64,128]{1,0:T(8,128)S(1)} collective-permute-done((f32[64,128]{1,0:T(8,128)S(1)}, f32[64,128]{1,0:T(8,128)S(1)}, u32[]{:S(2)}, u32[]{:S(2)}) %collective-permute-start.5) | collective-permute-done | bytes 32800 | tf_op jit(solution)/shard_map/ppermute | solution.py:264
  36.9 1.2 %collective-permute-start.6 = (f32[64,128]{1,0:T(8,128)S(1)}, f32[64,128]{1,0:T(8,128)S(1)}, u32[]{:S(2)}, u32[]{:S(2)}) collective-permute-start(f32[64,128]{1,0:T(8,128)S(1)} %add.31), channel_id=1, source_target_pairs={{0,32},{4,36},{8,40},{12,44},{16,48},{20,52},{24,56},{28,60},{32,0... | collective-permute-start | bytes 98312 | tf_op jit(solution)/shard_map/ppermute | solution.py:264
  38.1 2.6 %collective-permute-done.6 = f32[64,128]{1,0:T(8,128)S(1)} collective-permute-done((f32[64,128]{1,0:T(8,128)S(1)}, f32[64,128]{1,0:T(8,128)S(1)}, u32[]{:S(2)}, u32[]{:S(2)}) %collective-permute-start.6) | collective-permute-done | bytes 32800 | tf_op jit(solution)/shard_map/ppermute | solution.py:264
  40.7 0.0 collective-permute-done.13
  40.7 2.0 %collective-permute-start.14 = (f32[32,32,128]{2,1,0:T(8,128)S(1)}, f32[32,32,128]{2,1,0:T(8,128)S(1)}, u32[]{:S(2)}, u32[]{:S(2)}) collective-permute-start(f32[32,32,128]{2,1,0:T(8,128)S(1)} %pad_maximum_fusion.1), channel_id=1, source_target_pairs={{0,12},{4,8},{8,4},{12,0},{16,28},{20,24},{24,20},{28,16},{32,44},... | collective-permute-start | bytes 1572872 | tf_op jit(solution)/shard_map/ppermute | solution.py:247
  42.8 1.9 %collective-permute-start.7 = (f32[64,128]{1,0:T(8,128)S(1)}, f32[64,128]{1,0:T(8,128)S(1)}, u32[]{:S(2)}, u32[]{:S(2)}) collective-permute-start(f32[64,128]{1,0:T(8,128)S(1)} %add.32), channel_id=1, source_target_pairs={{0,96},{4,100},{8,104},{12,108},{16,112},{20,116},{24,120},{28,124... | collective-permute-start | bytes 98312 | tf_op jit(solution)/shard_map/ppermute | solution.py:264
  44.7 2.9 %collective-permute-done.7 = f32[64,128]{1,0:T(8,128)S(1)} collective-permute-done((f32[64,128]{1,0:T(8,128)S(1)}, f32[64,128]{1,0:T(8,128)S(1)}, u32[]{:S(2)}, u32[]{:S(2)}) %collective-permute-start.7) | collective-permute-done | bytes 32800 | tf_op jit(solution)/shard_map/ppermute | solution.py:264
  47.6 1.4 %collective-permute-start.8 = (f32[64,128]{1,0:T(8,128)S(1)}, f32[64,128]{1,0:T(8,128)S(1)}, u32[]{:S(2)}, u32[]{:S(2)}) collective-permute-start(f32[64,128]{1,0:T(8,128)S(1)} %add.33.fa_ref), channel_id=1, source_target_pairs={{0,128},{4,132},{8,136},{12,140},{16,144},{20,148},{24,152},{28,15... | collective-permute-start | bytes 98312 | tf_op jit(solution)/shard_map/ppermute | solution.py:265
  49.0 1.4 %collective-permute-done.8.fb_ref = f32[64,128]{1,0:T(8,128)S(1)} collective-permute-done((f32[64,128]{1,0:T(8,128)S(1)}, f32[64,128]{1,0:T(8,128)S(1)}, u32[]{:S(2)}, u32[]{:S(2)}) %collective-permute-start.8) | collective-permute-done | bytes 32800 | tf_op jit(solution)/shard_map/ppermute | solution.py:265
  50.4 2.8 %solve.1.solved_ref = f32[2,32,128]{2,1,0:T(8,128)S(1)} custom-call(f32[64,128]{1,0:T(8,128)S(1)} %add.33.fa_ref, f32[64,128]{1,0:T(8,128)S(1)} %collective-permute-done.8.fb_ref, f32[64,128]{1,0:T(8,128)S(1)} %get-tuple-element.23.grad_ref), custom_call_target="tpu_custom_call" | custom-call | bytes 8000000 | tf_op jit(solution)/shard_map/solve/pallas_call | solution.py:184
  53.2 0.0 collective-permute-done.14
  53.2 0.1 pad_maximum_fusion.q_ref
  53.3 0.8 %contract.1 = f32[2,64]{1,0:T(2,128)S(1)} custom-call(f32[2,32,128]{2,1,0:T(8,128)S(1)} %solve.1.solved_ref, f32[64,32,128]{2,1,0:T(8,128)S(1)} %pad_maximum_fusion.q_ref), custom_call_target="tpu_custom_call" | custom-call | tf_op jit(solution)/shard_map/contract/pallas_call | solution.py:227
  54.1 8.6 %collective-permute-start.15 = (f32[2,64]{1,0:T(2,128)S(1)}, f32[2,64]{1,0:T(2,128)S(1)}, u32[]{:S(2)}, u32[]{:S(2)}) collective-permute-start(f32[2,64]{1,0:T(2,128)S(1)} %contract.1), channel_id=1, source_target_pairs={{0,1},{1,0},{2,3},{3,2},{4,5},{5,4},{6,7},{7,6},{8,9},{9,8},{10,11... | collective-permute-start | bytes 1544 | tf_op jit(solution)/shard_map/ppermute | solution.py:269
  62.7 0.8 %collective-permute-done.15 = f32[2,64]{1,0:T(2,128)S(1)} collective-permute-done((f32[2,64]{1,0:T(2,128)S(1)}, f32[2,64]{1,0:T(2,128)S(1)}, u32[]{:S(2)}, u32[]{:S(2)}) %collective-permute-start.15) | collective-permute-done | bytes 544 | tf_op jit(solution)/shard_map/ppermute | solution.py:269
  63.5 1.6 %collective-permute-start.16 = (f32[2,64]{1,0:T(2,128)S(1)}, f32[2,64]{1,0:T(2,128)S(1)}, u32[]{:S(2)}, u32[]{:S(2)}) collective-permute-start(f32[2,64]{1,0:T(2,128)S(1)} %add.34), channel_id=1, source_target_pairs={{0,2},{1,3},{2,0},{3,1},{4,6},{5,7},{6,4},{7,5},{8,10},{9,11},{10,... | collective-permute-start | bytes 1544 | tf_op jit(solution)/shard_map/ppermute | solution.py:270
  65.1 2.3 %collective-permute-done.16 = f32[2,64]{1,0:T(2,128)S(1)} collective-permute-done((f32[2,64]{1,0:T(2,128)S(1)}, f32[2,64]{1,0:T(2,128)S(1)}, u32[]{:S(2)}, u32[]{:S(2)}) %collective-permute-start.16) | collective-permute-done | bytes 544 | tf_op jit(solution)/shard_map/ppermute | solution.py:270
  67.4 0.6 add.35
  (13 shorter events, 0.2 us)
Async XLA Ops:
  3.5 7.4 %collective-permute-start = (f32[512,128]{1,0:T(8,128)}, f32[512,128]{1,0:T(8,128)S(1)}, u32[]{:S(2)}, u32[]{:S(2)}) collective-permute-start(f32[512,128]{1,0:T(8,128)} %get-tuple-element.18), channel_id=1, source_target_pairs={{0,1},{1,0},{2,3},{3,2},{4,5},{5,4},{6,7},{7,6},{8,9},{9,8},{10,11... | collective-permute-start | bytes 786440 | tf_op jit(solution)/shard_map/ppermute | solution.py:251
  6.9 10.7 %collective-permute-start.9 = (f32[1,32,128]{2,1,0:T(8,128)S(1)}, f32[1,32,128]{2,1,0:T(8,128)S(1)}, u32[]{:S(2)}, u32[]{:S(2)}) collective-permute-start(f32[1,32,128]{2,1,0:T(8,128)S(1)} %get-tuple-element.25), channel_id=1, source_target_pairs={{0,32},{4,36},{8,40},{12,44},{16,48},{20,52},{24,56},{28,60},{32,0... | collective-permute-start | bytes 49160 | tf_op jit(solution)/shard_map/ppermute | solution.py:247
  11.0 14.4 %collective-permute-start.1 = (f32[512,128]{1,0:T(8,128)S(1)}, f32[512,128]{1,0:T(8,128)S(1)}, u32[]{:S(2)}, u32[]{:S(2)}) collective-permute-start(f32[512,128]{1,0:T(8,128)S(1)} %add.27), channel_id=1, source_target_pairs={{0,2},{1,3},{2,0},{3,1},{4,6},{5,7},{6,4},{7,5},{8,10},{9,11},{10,... | collective-permute-start | bytes 786440 | tf_op jit(solution)/shard_map/ppermute | solution.py:253
  16.8 8.6 %collective-permute-start.2 = (f32[512,128]{1,0:T(8,128)S(1)}, f32[512,128]{1,0:T(8,128)S(1)}, u32[]{:S(2)}, u32[]{:S(2)}) collective-permute-start(f32[512,128]{1,0:T(8,128)S(1)} %project.6), channel_id=1, source_target_pairs={{0,1},{1,0},{2,3},{3,2},{4,5},{5,4},{6,7},{7,6},{8,9},{9,8},{10,11... | collective-permute-start | bytes 786440 | tf_op jit(solution)/shard_map/ppermute | solution.py:255
  17.6 7.0 %collective-permute-start.10 = (f32[2,32,128]{2,1,0:T(8,128)S(1)}, f32[2,32,128]{2,1,0:T(8,128)S(1)}, u32[]{:S(2)}, u32[]{:S(2)}) collective-permute-start(f32[2,32,128]{2,1,0:T(8,128)S(1)} %pad_maximum_fusion.5), channel_id=1, source_target_pairs={{0,96},{4,100},{8,104},{12,108},{16,112},{20,116},{24,120},{28,124... | collective-permute-start | bytes 98312 | tf_op jit(solution)/shard_map/ppermute | solution.py:247
  24.6 3.2 %collective-permute-start.11 = (f32[4,32,128]{2,1,0:T(8,128)S(1)}, f32[4,32,128]{2,1,0:T(8,128)S(1)}, u32[]{:S(2)}, u32[]{:S(2)}) collective-permute-start(f32[4,32,128]{2,1,0:T(8,128)S(1)} %pad_maximum_fusion.4), channel_id=1, source_target_pairs={{0,16},{4,20},{8,24},{12,28},{16,0},{20,4},{24,8},{28,12},{32,48},... | collective-permute-start | bytes 196616 | tf_op jit(solution)/shard_map/ppermute | solution.py:247
  25.9 3.1 %collective-permute-start.3 = (f32[64,128]{1,0:T(8,128)S(1)}, f32[64,128]{1,0:T(8,128)S(1)}, u32[]{:S(2)}, u32[]{:S(2)}) collective-permute-start(f32[64,128]{1,0:T(8,128)S(1)} %get-tuple-element.22), channel_id=1, source_target_pairs={{0,4},{4,0},{8,12},{12,8},{16,20},{20,16},{24,28},{28,24},{32,36},... | collective-permute-start | bytes 98312 | tf_op jit(solution)/shard_map/ppermute | solution.py:264
  29.0 4.4 %collective-permute-start.12 = (f32[8,32,128]{2,1,0:T(8,128)S(1)}, f32[8,32,128]{2,1,0:T(8,128)S(1)}, u32[]{:S(2)}, u32[]{:S(2)}) collective-permute-start(f32[8,32,128]{2,1,0:T(8,128)S(1)} %pad_maximum_fusion.3), channel_id=1, source_target_pairs={{0,128},{4,132},{8,136},{12,140},{16,144},{20,148},{24,152},{28,15... | collective-permute-start | bytes 393224 | tf_op jit(solution)/shard_map/ppermute | solution.py:247
  29.4 4.0 %collective-permute-start.4 = (f32[64,128]{1,0:T(8,128)S(1)}, f32[64,128]{1,0:T(8,128)S(1)}, u32[]{:S(2)}, u32[]{:S(2)}) collective-permute-start(f32[64,128]{1,0:T(8,128)S(1)} %add.29), channel_id=1, source_target_pairs={{0,12},{4,8},{8,4},{12,0},{16,28},{20,24},{24,20},{28,16},{32,44},... | collective-permute-start | bytes 98312 | tf_op jit(solution)/shard_map/ppermute | solution.py:264
  33.4 7.3 %collective-permute-start.13 = (f32[16,32,128]{2,1,0:T(8,128)S(1)}, f32[16,32,128]{2,1,0:T(8,128)S(1)}, u32[]{:S(2)}, u32[]{:S(2)}) collective-permute-start(f32[16,32,128]{2,1,0:T(8,128)S(1)} %pad_maximum_fusion.2), channel_id=1, source_target_pairs={{0,4},{4,0},{8,12},{12,8},{16,20},{20,16},{24,28},{28,24},{32,36},... | collective-permute-start | bytes 786440 | tf_op jit(solution)/shard_map/ppermute | solution.py:247
  34.1 2.8 %collective-permute-start.5 = (f32[64,128]{1,0:T(8,128)S(1)}, f32[64,128]{1,0:T(8,128)S(1)}, u32[]{:S(2)}, u32[]{:S(2)}) collective-permute-start(f32[64,128]{1,0:T(8,128)S(1)} %add.30), channel_id=1, source_target_pairs={{0,16},{4,20},{8,24},{12,28},{16,0},{20,4},{24,8},{28,12},{32,48},... | collective-permute-start | bytes 98312 | tf_op jit(solution)/shard_map/ppermute | solution.py:264
  36.9 3.8 %collective-permute-start.6 = (f32[64,128]{1,0:T(8,128)S(1)}, f32[64,128]{1,0:T(8,128)S(1)}, u32[]{:S(2)}, u32[]{:S(2)}) collective-permute-start(f32[64,128]{1,0:T(8,128)S(1)} %add.31), channel_id=1, source_target_pairs={{0,32},{4,36},{8,40},{12,44},{16,48},{20,52},{24,56},{28,60},{32,0... | collective-permute-start | bytes 98312 | tf_op jit(solution)/shard_map/ppermute | solution.py:264
  40.7 12.5 %collective-permute-start.14 = (f32[32,32,128]{2,1,0:T(8,128)S(1)}, f32[32,32,128]{2,1,0:T(8,128)S(1)}, u32[]{:S(2)}, u32[]{:S(2)}) collective-permute-start(f32[32,32,128]{2,1,0:T(8,128)S(1)} %pad_maximum_fusion.1), channel_id=1, source_target_pairs={{0,12},{4,8},{8,4},{12,0},{16,28},{20,24},{24,20},{28,16},{32,44},... | collective-permute-start | bytes 1572872 | tf_op jit(solution)/shard_map/ppermute | solution.py:247
  42.8 4.9 %collective-permute-start.7 = (f32[64,128]{1,0:T(8,128)S(1)}, f32[64,128]{1,0:T(8,128)S(1)}, u32[]{:S(2)}, u32[]{:S(2)}) collective-permute-start(f32[64,128]{1,0:T(8,128)S(1)} %add.32), channel_id=1, source_target_pairs={{0,96},{4,100},{8,104},{12,108},{16,112},{20,116},{24,120},{28,124... | collective-permute-start | bytes 98312 | tf_op jit(solution)/shard_map/ppermute | solution.py:264
  47.6 2.8 %collective-permute-start.8 = (f32[64,128]{1,0:T(8,128)S(1)}, f32[64,128]{1,0:T(8,128)S(1)}, u32[]{:S(2)}, u32[]{:S(2)}) collective-permute-start(f32[64,128]{1,0:T(8,128)S(1)} %add.33.fa_ref), channel_id=1, source_target_pairs={{0,128},{4,132},{8,136},{12,140},{16,144},{20,148},{24,152},{28,15... | collective-permute-start | bytes 98312 | tf_op jit(solution)/shard_map/ppermute | solution.py:265
  54.1 9.4 %collective-permute-start.15 = (f32[2,64]{1,0:T(2,128)S(1)}, f32[2,64]{1,0:T(2,128)S(1)}, u32[]{:S(2)}, u32[]{:S(2)}) collective-permute-start(f32[2,64]{1,0:T(2,128)S(1)} %contract.1), channel_id=1, source_target_pairs={{0,1},{1,0},{2,3},{3,2},{4,5},{5,4},{6,7},{7,6},{8,9},{9,8},{10,11... | collective-permute-start | bytes 1544 | tf_op jit(solution)/shard_map/ppermute | solution.py:269
  63.5 3.9 %collective-permute-start.16 = (f32[2,64]{1,0:T(2,128)S(1)}, f32[2,64]{1,0:T(2,128)S(1)}, u32[]{:S(2)}, u32[]{:S(2)}) collective-permute-start(f32[2,64]{1,0:T(2,128)S(1)} %add.34), channel_id=1, source_target_pairs={{0,2},{1,3},{2,0},{3,1},{4,6},{5,7},{6,4},{7,5},{8,10},{9,11},{10,... | collective-permute-start | bytes 1544 | tf_op jit(solution)/shard_map/ppermute | solution.py:270

commit v2 on v1

--- a/solution.py
+++ b/solution.py
@@ -10,9 +10,9 @@
 DAMP = 0.1
 QUERY_VMEM = 56426496
 VMEM = 53 * 2**20 + 2**19
-QUERY_BITS = (8, 24, 4, 32, 1, 3)
+QUERY_BITS = (8, 4, 24, 32, 1, 3)
 QUERY_AT = {1: 3, 2: 4, 4: 5}
-FACTOR_BITS = (1, 3, 4, 8, 24, 32)
+FACTOR_BITS = (1, 3, 4, 24, 8, 32)
 HIGH = lax.Precision.HIGHEST
 
 
@@ -40,12 +40,14 @@
         fetch.start()
     for copy in copies:
         copy.start()
-    for copy in copies:
-        copy.wait()
     contract = (((1,), (1,)), ((), ()))
+    copies[0].wait()
+    copies[1].wait()
     out[:, :rank] = lax.dot_general(
         xs[...].reshape(rows, xs.shape[2]), pis[...], contract, preferred_element_type=jnp.float32
     )
+    copies[2].wait()
+    copies[3].wait()
     out[:, rank:] = lax.dot_general(
         gs[...].reshape(rows, gs.shape[2]), pos[...], contract, preferred_element_type=jnp.float32
     )

time: 68.2 us -> 67.5 us (0.990)
  waiting for transfers between devices: 15.3 us -> 13.6 us
  starting transfers between devices: 35.8 us -> 36.7 us
    ppermute x5, starting transfers between devices: 7.66 us -> 9.81 us  [local(): fac = fac + lax.ppermute(fac, 'dp', xor_pairs(groups, bit))]
    ppermute x5, waiting for transfers between devices: 10.2 us -> 8.59 us  [local(): fac = fac + lax.ppermute(fac, 'dp', xor_pairs(groups, bit))]
    ppermute x1, starting transfers between devices: 8.57 us -> 7.77 us  [local(): out = out + lax.ppermute(out, 'mp', xor_pairs(members, 1))]
where the time goes in v2:
time: 67.5 us; the launch traced here: 67.3 us
  starting transfers between devices  36.7 us (54%)
  Pallas kernels  16 us (24%)
  waiting for transfers between devices  13.6 us (20%)
  other arithmetic  0.8 us (1%)
    pallas_call x4, Pallas kernels, project(): pl.pallas_call(functools.partial(project_kernel, offset, query is not Non...  12 us
    ppermute x5, starting transfers between devices, local(): fac = fac + lax.ppermute(fac, 'dp', xor_pairs(groups, bit))  9.81 us
    ppermute x6, starting transfers between devices, widen(): return jnp.concatenate([blocks, lax.ppermute(blocks, 'dp', pairs)])  9.43 us
    ppermute x5, waiting for transfers between devices, local(): fac = fac + lax.ppermute(fac, 'dp', xor_pairs(groups, bit))  8.59 us
    ppermute x1, starting transfers between devices, local(): out = out + lax.ppermute(out, 'mp', xor_pairs(members, 1))  7.77 us
    ppermute x1, starting transfers between devices, local(): far_in = lax.ppermute(far, 'mp', xor_pairs(members, 1))  3.33 us
    ppermute x1, starting transfers between devices, local(): cross_in = lax.ppermute(cross, 'mp', xor_pairs(members, 2))  3.01 us
    pallas_call x1, Pallas kernels, solve(): pl.pallas_call(functools.partial(solve_kernel, clips, total), in_specs=[v...  2.81 us
  transfers between devices with their start and end apart: 17, of which 9 were waited for; matrix products, arithmetic and copies ran while one was open for 0% of the time, Pallas kernels for 17%

profile of v2, /device:TPU:1, one launch (start us, length us, event | category | flops | bytes accessed | tf_op | source)
XLA Modules:
  0.0 67.3 jit_solution(14692435509569166012)
XLA Ops:
  0.0 3.5 %project.4 = (f32[512,128]{1,0:T(8,128)}, f32[1,32,128]{2,1,0:T(8,128)S(1)}) custom-call(bf16[4,2,256,512]{3,2,1,0:T(8,128)(2,1)} %x_hbm.7, bf16[4,2,256,2048]{3,2,1,0:T(8,128)(2,1)} %g_hbm.7, bf16[4,64,512]{2,1,0:T(8,128)(2,1)} %pi_hbm.4, bf16[4,64,2048]{2,1,0:T(8,128)(2,1)} %po_hbm.7, f32[4,1,64,64]{3,2,1,0:T(8,128)} %rest_0_.1), custom_call_target="tpu_custom_call" | custom-call | flops 167772160 | bytes 2883584 | tf_op jit(solution)/shard_map/project/pallas_call | solution.py:85
  3.5 3.3 %collective-permute-start = (f32[512,128]{1,0:T(8,128)}, f32[512,128]{1,0:T(8,128)S(1)}, u32[]{:S(2)}, u32[]{:S(2)}) collective-permute-start(f32[512,128]{1,0:T(8,128)} %get-tuple-element.18), channel_id=1, source_target_pairs={{0,1},{1,0},{2,3},{3,2},{4,5},{5,4},{6,7},{7,6},{8,9},{9,8},{10,11... | collective-permute-start | bytes 786440 | tf_op jit(solution)/shard_map/ppermute | solution.py:253
  6.9 1.3 %collective-permute-start.9 = (f32[1,32,128]{2,1,0:T(8,128)S(1)}, f32[1,32,128]{2,1,0:T(8,128)S(1)}, u32[]{:S(2)}, u32[]{:S(2)}) collective-permute-start(f32[1,32,128]{2,1,0:T(8,128)S(1)} %get-tuple-element.25), channel_id=1, source_target_pairs={{0,32},{4,36},{8,40},{12,44},{16,48},{20,52},{24,56},{28,60},{32,0... | collective-permute-start | bytes 49160 | tf_op jit(solution)/shard_map/ppermute | solution.py:249
  8.1 2.8 %project.5 = f32[512,128]{1,0:T(8,128)S(1)} custom-call(bf16[4,2,256,512]{3,2,1,0:T(8,128)(2,1)} %x_hbm.7, bf16[4,2,256,2048]{3,2,1,0:T(8,128)(2,1)} %g_hbm.7, bf16[4,64,512]{2,1,0:T(8,128)(2,1)} %pi_hbm.4, bf16[4,64,2048]{2,1,0:T(8,128)(2,1)} %po_hbm.7), custom_call_target="tpu_custom_call" | custom-call | flops 167772160 | bytes 2883584 | tf_op jit(solution)/shard_map/project/pallas_call | solution.py:85
  11.0 0.0 collective-permute-done
  11.0 3.0 %collective-permute-start.1 = (f32[512,128]{1,0:T(8,128)S(1)}, f32[512,128]{1,0:T(8,128)S(1)}, u32[]{:S(2)}, u32[]{:S(2)}) collective-permute-start(f32[512,128]{1,0:T(8,128)S(1)} %add.27), channel_id=1, source_target_pairs={{0,2},{1,3},{2,0},{3,1},{4,6},{5,7},{6,4},{7,5},{8,10},{9,11},{10,... | collective-permute-start | bytes 786440 | tf_op jit(solution)/shard_map/ppermute | solution.py:255
  14.0 2.8 %project.6 = f32[512,128]{1,0:T(8,128)S(1)} custom-call(bf16[4,2,256,512]{3,2,1,0:T(8,128)(2,1)} %x_hbm.7, bf16[4,2,256,2048]{3,2,1,0:T(8,128)(2,1)} %g_hbm.7, bf16[4,64,512]{2,1,0:T(8,128)(2,1)} %pi_hbm.4, bf16[4,64,2048]{2,1,0:T(8,128)(2,1)} %po_hbm.7), custom_call_target="tpu_custom_call" | custom-call | flops 167772160 | bytes 2883584 | tf_op jit(solution)/shard_map/project/pallas_call | solution.py:85
  16.8 0.7 %collective-permute-start.2 = (f32[512,128]{1,0:T(8,128)S(1)}, f32[512,128]{1,0:T(8,128)S(1)}, u32[]{:S(2)}, u32[]{:S(2)}) collective-permute-start(f32[512,128]{1,0:T(8,128)S(1)} %project.6), channel_id=1, source_target_pairs={{0,1},{1,0},{2,3},{3,2},{4,5},{5,4},{6,7},{7,6},{8,9},{9,8},{10,11... | collective-permute-start | bytes 786440 | tf_op jit(solution)/shard_map/ppermute | solution.py:257
  17.6 0.0 collective-permute-done.9
  17.6 1.6 %collective-permute-start.10 = (f32[2,32,128]{2,1,0:T(8,128)S(1)}, f32[2,32,128]{2,1,0:T(8,128)S(1)}, u32[]{:S(2)}, u32[]{:S(2)}) collective-permute-start(f32[2,32,128]{2,1,0:T(8,128)S(1)} %pad_maximum_fusion.5), channel_id=1, source_target_pairs={{0,16},{4,20},{8,24},{12,28},{16,0},{20,4},{24,8},{28,12},{32,48},... | collective-permute-start | bytes 98312 | tf_op jit(solution)/shard_map/ppermute | solution.py:249
  19.2 2.8 %project.7 = f32[512,128]{1,0:T(8,128)S(1)} custom-call(bf16[4,2,256,512]{3,2,1,0:T(8,128)(2,1)} %x_hbm.7, bf16[4,2,256,2048]{3,2,1,0:T(8,128)(2,1)} %g_hbm.7, bf16[4,64,512]{2,1,0:T(8,128)(2,1)} %pi_hbm.4, bf16[4,64,2048]{2,1,0:T(8,128)(2,1)} %po_hbm.7), custom_call_target="tpu_custom_call" | custom-call | flops 167772160 | bytes 2883584 | tf_op jit(solution)/shard_map/project/pallas_call | solution.py:85
  22.0 0.0 collective-permute-done.10
  22.0 3.4 %collective-permute-start.11 = (f32[4,32,128]{2,1,0:T(8,128)S(1)}, f32[4,32,128]{2,1,0:T(8,128)S(1)}, u32[]{:S(2)}, u32[]{:S(2)}) collective-permute-start(f32[4,32,128]{2,1,0:T(8,128)S(1)} %pad_maximum_fusion.4), channel_id=1, source_target_pairs={{0,96},{4,100},{8,104},{12,108},{16,112},{20,116},{24,120},{28,124... | collective-permute-start | bytes 196616 | tf_op jit(solution)/shard_map/ppermute | solution.py:249
  25.4 0.0 collective-permute-done.1
  25.5 0.0 collective-permute-done.2.b_ref
  25.5 0.4 moments.1
  25.9 1.3 %collective-permute-start.3 = (f32[64,128]{1,0:T(8,128)S(1)}, f32[64,128]{1,0:T(8,128)S(1)}, u32[]{:S(2)}, u32[]{:S(2)}) collective-permute-start(f32[64,128]{1,0:T(8,128)S(1)} %get-tuple-element.22), channel_id=1, source_target_pairs={{0,4},{4,0},{8,12},{12,8},{16,20},{20,16},{24,28},{28,24},{32,36},... | collective-permute-start | bytes 98312 | tf_op jit(solution)/shard_map/ppermute | solution.py:266
  27.2 0.2 collective-permute-done.11
  27.4 1.4 %collective-permute-done.3 = f32[64,128]{1,0:T(8,128)S(1)} collective-permute-done((f32[64,128]{1,0:T(8,128)S(1)}, f32[64,128]{1,0:T(8,128)S(1)}, u32[]{:S(2)}, u32[]{:S(2)}) %collective-permute-start.3) | collective-permute-done | bytes 32800 | tf_op jit(solution)/shard_map/ppermute | solution.py:266
  28.8 0.4 collective-permute-start.12
  29.2 2.5 %collective-permute-start.4 = (f32[64,128]{1,0:T(8,128)S(1)}, f32[64,128]{1,0:T(8,128)S(1)}, u32[]{:S(2)}, u32[]{:S(2)}) collective-permute-start(f32[64,128]{1,0:T(8,128)S(1)} %add.29), channel_id=1, source_target_pairs={{0,12},{4,8},{8,4},{12,0},{16,28},{20,24},{24,20},{28,16},{32,44},... | collective-permute-start | bytes 98312 | tf_op jit(solution)/shard_map/ppermute | solution.py:266
  31.6 1.5 %collective-permute-done.4 = f32[64,128]{1,0:T(8,128)S(1)} collective-permute-done((f32[64,128]{1,0:T(8,128)S(1)}, f32[64,128]{1,0:T(8,128)S(1)}, u32[]{:S(2)}, u32[]{:S(2)}) %collective-permute-start.4) | collective-permute-done | bytes 32800 | tf_op jit(solution)/shard_map/ppermute | solution.py:266
  33.1 0.0 collective-permute-done.12
  33.2 0.7 %collective-permute-start.13 = (f32[16,32,128]{2,1,0:T(8,128)S(1)}, f32[16,32,128]{2,1,0:T(8,128)S(1)}, u32[]{:S(2)}, u32[]{:S(2)}) collective-permute-start(f32[16,32,128]{2,1,0:T(8,128)S(1)} %pad_maximum_fusion.2), channel_id=1, source_target_pairs={{0,4},{4,0},{8,12},{12,8},{16,20},{20,16},{24,28},{28,24},{32,36},... | collective-permute-start | bytes 786440 | tf_op jit(solution)/shard_map/ppermute | solution.py:249
  33.9 1.0 %collective-permute-start.5 = (f32[64,128]{1,0:T(8,128)S(1)}, f32[64,128]{1,0:T(8,128)S(1)}, u32[]{:S(2)}, u32[]{:S(2)}) collective-permute-start(f32[64,128]{1,0:T(8,128)S(1)} %add.30), channel_id=1, source_target_pairs={{0,16},{4,20},{8,24},{12,28},{16,0},{20,4},{24,8},{28,12},{32,48},... | collective-permute-start | bytes 98312 | tf_op jit(solution)/shard_map/ppermute | solution.py:266
  34.9 1.7 %collective-permute-done.5 = f32[64,128]{1,0:T(8,128)S(1)} collective-permute-done((f32[64,128]{1,0:T(8,128)S(1)}, f32[64,128]{1,0:T(8,128)S(1)}, u32[]{:S(2)}, u32[]{:S(2)}) %collective-permute-start.5) | collective-permute-done | bytes 32800 | tf_op jit(solution)/shard_map/ppermute | solution.py:266
  36.7 3.9 %collective-permute-start.6 = (f32[64,128]{1,0:T(8,128)S(1)}, f32[64,128]{1,0:T(8,128)S(1)}, u32[]{:S(2)}, u32[]{:S(2)}) collective-permute-start(f32[64,128]{1,0:T(8,128)S(1)} %add.31), channel_id=1, source_target_pairs={{0,96},{4,100},{8,104},{12,108},{16,112},{20,116},{24,120},{28,124... | collective-permute-start | bytes 98312 | tf_op jit(solution)/shard_map/ppermute | solution.py:266
  40.6 1.4 %collective-permute-done.6 = f32[64,128]{1,0:T(8,128)S(1)} collective-permute-done((f32[64,128]{1,0:T(8,128)S(1)}, f32[64,128]{1,0:T(8,128)S(1)}, u32[]{:S(2)}, u32[]{:S(2)}) %collective-permute-start.6) | collective-permute-done | bytes 32800 | tf_op jit(solution)/shard_map/ppermute | solution.py:266
  42.0 0.0 collective-permute-done.13
  42.1 2.0 %collective-permute-start.14 = (f32[32,32,128]{2,1,0:T(8,128)S(1)}, f32[32,32,128]{2,1,0:T(8,128)S(1)}, u32[]{:S(2)}, u32[]{:S(2)}) collective-permute-start(f32[32,32,128]{2,1,0:T(8,128)S(1)} %pad_maximum_fusion.1), channel_id=1, source_target_pairs={{0,12},{4,8},{8,4},{12,0},{16,28},{20,24},{24,20},{28,16},{32,44},... | collective-permute-start | bytes 1572872 | tf_op jit(solution)/shard_map/ppermute | solution.py:249
  44.1 1.1 %collective-permute-start.7 = (f32[64,128]{1,0:T(8,128)S(1)}, f32[64,128]{1,0:T(8,128)S(1)}, u32[]{:S(2)}, u32[]{:S(2)}) collective-permute-start(f32[64,128]{1,0:T(8,128)S(1)} %add.32), channel_id=1, source_target_pairs={{0,32},{4,36},{8,40},{12,44},{16,48},{20,52},{24,56},{28,60},{32,0... | collective-permute-start | bytes 98312 | tf_op jit(solution)/shard_map/ppermute | solution.py:266
  45.2 2.6 %collective-permute-done.7 = f32[64,128]{1,0:T(8,128)S(1)} collective-permute-done((f32[64,128]{1,0:T(8,128)S(1)}, f32[64,128]{1,0:T(8,128)S(1)}, u32[]{:S(2)}, u32[]{:S(2)}) %collective-permute-start.7) | collective-permute-done | bytes 32800 | tf_op jit(solution)/shard_map/ppermute | solution.py:266
  47.7 1.1 %collective-permute-start.8 = (f32[64,128]{1,0:T(8,128)S(1)}, f32[64,128]{1,0:T(8,128)S(1)}, u32[]{:S(2)}, u32[]{:S(2)}) collective-permute-start(f32[64,128]{1,0:T(8,128)S(1)} %add.33.fa_ref), channel_id=1, source_target_pairs={{0,128},{4,132},{8,136},{12,140},{16,144},{20,148},{24,152},{28,15... | collective-permute-start | bytes 98312 | tf_op jit(solution)/shard_map/ppermute | solution.py:267
  48.8 1.7 %collective-permute-done.8.fb_ref = f32[64,128]{1,0:T(8,128)S(1)} collective-permute-done((f32[64,128]{1,0:T(8,128)S(1)}, f32[64,128]{1,0:T(8,128)S(1)}, u32[]{:S(2)}, u32[]{:S(2)}) %collective-permute-start.8) | collective-permute-done | bytes 32800 | tf_op jit(solution)/shard_map/ppermute | solution.py:267
  50.5 2.8 %solve.1.solved_ref = f32[2,32,128]{2,1,0:T(8,128)S(1)} custom-call(f32[64,128]{1,0:T(8,128)S(1)} %add.33.fa_ref, f32[64,128]{1,0:T(8,128)S(1)} %collective-permute-done.8.fb_ref, f32[64,128]{1,0:T(8,128)S(1)} %get-tuple-element.23.grad_ref), custom_call_target="tpu_custom_call" | custom-call | bytes 8000000 | tf_op jit(solution)/shard_map/solve/pallas_call | solution.py:186
  53.3 0.0 collective-permute-done.14
  53.3 0.1 pad_maximum_fusion.q_ref
  53.4 0.8 %contract.1 = f32[2,64]{1,0:T(2,128)S(1)} custom-call(f32[2,32,128]{2,1,0:T(8,128)S(1)} %solve.1.solved_ref, f32[64,32,128]{2,1,0:T(8,128)S(1)} %pad_maximum_fusion.q_ref), custom_call_target="tpu_custom_call" | custom-call | tf_op jit(solution)/shard_map/contract/pallas_call | solution.py:229
  54.2 7.8 %collective-permute-start.15 = (f32[2,64]{1,0:T(2,128)S(1)}, f32[2,64]{1,0:T(2,128)S(1)}, u32[]{:S(2)}, u32[]{:S(2)}) collective-permute-start(f32[2,64]{1,0:T(2,128)S(1)} %contract.1), channel_id=1, source_target_pairs={{0,1},{1,0},{2,3},{3,2},{4,5},{5,4},{6,7},{7,6},{8,9},{9,8},{10,11... | collective-permute-start | bytes 1544 | tf_op jit(solution)/shard_map/ppermute | solution.py:271
  62.0 0.8 %collective-permute-done.15 = f32[2,64]{1,0:T(2,128)S(1)} collective-permute-done((f32[2,64]{1,0:T(2,128)S(1)}, f32[2,64]{1,0:T(2,128)S(1)}, u32[]{:S(2)}, u32[]{:S(2)}) %collective-permute-start.15) | collective-permute-done | bytes 544 | tf_op jit(solution)/shard_map/ppermute | solution.py:271
  62.8 1.6 %collective-permute-start.16 = (f32[2,64]{1,0:T(2,128)S(1)}, f32[2,64]{1,0:T(2,128)S(1)}, u32[]{:S(2)}, u32[]{:S(2)}) collective-permute-start(f32[2,64]{1,0:T(2,128)S(1)} %add.34), channel_id=1, source_target_pairs={{0,2},{1,3},{2,0},{3,1},{4,6},{5,7},{6,4},{7,5},{8,10},{9,11},{10,... | collective-permute-start | bytes 1544 | tf_op jit(solution)/shard_map/ppermute | solution.py:272
  64.4 2.4 %collective-permute-done.16 = f32[2,64]{1,0:T(2,128)S(1)} collective-permute-done((f32[2,64]{1,0:T(2,128)S(1)}, f32[2,64]{1,0:T(2,128)S(1)}, u32[]{:S(2)}, u32[]{:S(2)}) %collective-permute-start.16) | collective-permute-done | bytes 544 | tf_op jit(solution)/shard_map/ppermute | solution.py:272
  66.8 0.6 add.35
  (13 shorter events, 0.2 us)
Async XLA Ops:
  3.5 7.4 %collective-permute-start = (f32[512,128]{1,0:T(8,128)}, f32[512,128]{1,0:T(8,128)S(1)}, u32[]{:S(2)}, u32[]{:S(2)}) collective-permute-start(f32[512,128]{1,0:T(8,128)} %get-tuple-element.18), channel_id=1, source_target_pairs={{0,1},{1,0},{2,3},{3,2},{4,5},{5,4},{6,7},{7,6},{8,9},{9,8},{10,11... | collective-permute-start | bytes 786440 | tf_op jit(solution)/shard_map/ppermute | solution.py:253
  6.9 10.7 %collective-permute-start.9 = (f32[1,32,128]{2,1,0:T(8,128)S(1)}, f32[1,32,128]{2,1,0:T(8,128)S(1)}, u32[]{:S(2)}, u32[]{:S(2)}) collective-permute-start(f32[1,32,128]{2,1,0:T(8,128)S(1)} %get-tuple-element.25), channel_id=1, source_target_pairs={{0,32},{4,36},{8,40},{12,44},{16,48},{20,52},{24,56},{28,60},{32,0... | collective-permute-start | bytes 49160 | tf_op jit(solution)/shard_map/ppermute | solution.py:249
  11.0 14.4 %collective-permute-start.1 = (f32[512,128]{1,0:T(8,128)S(1)}, f32[512,128]{1,0:T(8,128)S(1)}, u32[]{:S(2)}, u32[]{:S(2)}) collective-permute-start(f32[512,128]{1,0:T(8,128)S(1)} %add.27), channel_id=1, source_target_pairs={{0,2},{1,3},{2,0},{3,1},{4,6},{5,7},{6,4},{7,5},{8,10},{9,11},{10,... | collective-permute-start | bytes 786440 | tf_op jit(solution)/shard_map/ppermute | solution.py:255
  16.8 8.6 %collective-permute-start.2 = (f32[512,128]{1,0:T(8,128)S(1)}, f32[512,128]{1,0:T(8,128)S(1)}, u32[]{:S(2)}, u32[]{:S(2)}) collective-permute-start(f32[512,128]{1,0:T(8,128)S(1)} %project.6), channel_id=1, source_target_pairs={{0,1},{1,0},{2,3},{3,2},{4,5},{5,4},{6,7},{7,6},{8,9},{9,8},{10,11... | collective-permute-start | bytes 786440 | tf_op jit(solution)/shard_map/ppermute | solution.py:257
  17.6 4.5 %collective-permute-start.10 = (f32[2,32,128]{2,1,0:T(8,128)S(1)}, f32[2,32,128]{2,1,0:T(8,128)S(1)}, u32[]{:S(2)}, u32[]{:S(2)}) collective-permute-start(f32[2,32,128]{2,1,0:T(8,128)S(1)} %pad_maximum_fusion.5), channel_id=1, source_target_pairs={{0,16},{4,20},{8,24},{12,28},{16,0},{20,4},{24,8},{28,12},{32,48},... | collective-permute-start | bytes 98312 | tf_op jit(solution)/shard_map/ppermute | solution.py:249
  22.0 5.3 %collective-permute-start.11 = (f32[4,32,128]{2,1,0:T(8,128)S(1)}, f32[4,32,128]{2,1,0:T(8,128)S(1)}, u32[]{:S(2)}, u32[]{:S(2)}) collective-permute-start(f32[4,32,128]{2,1,0:T(8,128)S(1)} %pad_maximum_fusion.4), channel_id=1, source_target_pairs={{0,96},{4,100},{8,104},{12,108},{16,112},{20,116},{24,120},{28,124... | collective-permute-start | bytes 196616 | tf_op jit(solution)/shard_map/ppermute | solution.py:249
  25.9 2.9 %collective-permute-start.3 = (f32[64,128]{1,0:T(8,128)S(1)}, f32[64,128]{1,0:T(8,128)S(1)}, u32[]{:S(2)}, u32[]{:S(2)}) collective-permute-start(f32[64,128]{1,0:T(8,128)S(1)} %get-tuple-element.22), channel_id=1, source_target_pairs={{0,4},{4,0},{8,12},{12,8},{16,20},{20,16},{24,28},{28,24},{32,36},... | collective-permute-start | bytes 98312 | tf_op jit(solution)/shard_map/ppermute | solution.py:266
  28.8 4.4 %collective-permute-start.12 = (f32[8,32,128]{2,1,0:T(8,128)S(1)}, f32[8,32,128]{2,1,0:T(8,128)S(1)}, u32[]{:S(2)}, u32[]{:S(2)}) collective-permute-start(f32[8,32,128]{2,1,0:T(8,128)S(1)} %pad_maximum_fusion.3), channel_id=1, source_target_pairs={{0,128},{4,132},{8,136},{12,140},{16,144},{20,148},{24,152},{28,15... | collective-permute-start | bytes 393224 | tf_op jit(solution)/shard_map/ppermute | solution.py:249
  29.2 4.0 %collective-permute-start.4 = (f32[64,128]{1,0:T(8,128)S(1)}, f32[64,128]{1,0:T(8,128)S(1)}, u32[]{:S(2)}, u32[]{:S(2)}) collective-permute-start(f32[64,128]{1,0:T(8,128)S(1)} %add.29), channel_id=1, source_target_pairs={{0,12},{4,8},{8,4},{12,0},{16,28},{20,24},{24,20},{28,16},{32,44},... | collective-permute-start | bytes 98312 | tf_op jit(solution)/shard_map/ppermute | solution.py:266
  33.2 8.8 %collective-permute-start.13 = (f32[16,32,128]{2,1,0:T(8,128)S(1)}, f32[16,32,128]{2,1,0:T(8,128)S(1)}, u32[]{:S(2)}, u32[]{:S(2)}) collective-permute-start(f32[16,32,128]{2,1,0:T(8,128)S(1)} %pad_maximum_fusion.2), channel_id=1, source_target_pairs={{0,4},{4,0},{8,12},{12,8},{16,20},{20,16},{24,28},{28,24},{32,36},... | collective-permute-start | bytes 786440 | tf_op jit(solution)/shard_map/ppermute | solution.py:249
  33.9 2.8 %collective-permute-start.5 = (f32[64,128]{1,0:T(8,128)S(1)}, f32[64,128]{1,0:T(8,128)S(1)}, u32[]{:S(2)}, u32[]{:S(2)}) collective-permute-start(f32[64,128]{1,0:T(8,128)S(1)} %add.30), channel_id=1, source_target_pairs={{0,16},{4,20},{8,24},{12,28},{16,0},{20,4},{24,8},{28,12},{32,48},... | collective-permute-start | bytes 98312 | tf_op jit(solution)/shard_map/ppermute | solution.py:266
  36.7 5.3 %collective-permute-start.6 = (f32[64,128]{1,0:T(8,128)S(1)}, f32[64,128]{1,0:T(8,128)S(1)}, u32[]{:S(2)}, u32[]{:S(2)}) collective-permute-start(f32[64,128]{1,0:T(8,128)S(1)} %add.31), channel_id=1, source_target_pairs={{0,96},{4,100},{8,104},{12,108},{16,112},{20,116},{24,120},{28,124... | collective-permute-start | bytes 98312 | tf_op jit(solution)/shard_map/ppermute | solution.py:266
  42.1 11.3 %collective-permute-start.14 = (f32[32,32,128]{2,1,0:T(8,128)S(1)}, f32[32,32,128]{2,1,0:T(8,128)S(1)}, u32[]{:S(2)}, u32[]{:S(2)}) collective-permute-start(f32[32,32,128]{2,1,0:T(8,128)S(1)} %pad_maximum_fusion.1), channel_id=1, source_target_pairs={{0,12},{4,8},{8,4},{12,0},{16,28},{20,24},{24,20},{28,16},{32,44},... | collective-permute-start | bytes 1572872 | tf_op jit(solution)/shard_map/ppermute | solution.py:249
  44.1 3.7 %collective-permute-start.7 = (f32[64,128]{1,0:T(8,128)S(1)}, f32[64,128]{1,0:T(8,128)S(1)}, u32[]{:S(2)}, u32[]{:S(2)}) collective-permute-start(f32[64,128]{1,0:T(8,128)S(1)} %add.32), channel_id=1, source_target_pairs={{0,32},{4,36},{8,40},{12,44},{16,48},{20,52},{24,56},{28,60},{32,0... | collective-permute-start | bytes 98312 | tf_op jit(solution)/shard_map/ppermute | solution.py:266
  47.7 2.8 %collective-permute-start.8 = (f32[64,128]{1,0:T(8,128)S(1)}, f32[64,128]{1,0:T(8,128)S(1)}, u32[]{:S(2)}, u32[]{:S(2)}) collective-permute-start(f32[64,128]{1,0:T(8,128)S(1)} %add.33.fa_ref), channel_id=1, source_target_pairs={{0,128},{4,132},{8,136},{12,140},{16,144},{20,148},{24,152},{28,15... | collective-permute-start | bytes 98312 | tf_op jit(solution)/shard_map/ppermute | solution.py:267
  54.2 8.6 %collective-permute-start.15 = (f32[2,64]{1,0:T(2,128)S(1)}, f32[2,64]{1,0:T(2,128)S(1)}, u32[]{:S(2)}, u32[]{:S(2)}) collective-permute-start(f32[2,64]{1,0:T(2,128)S(1)} %contract.1), channel_id=1, source_target_pairs={{0,1},{1,0},{2,3},{3,2},{4,5},{5,4},{6,7},{7,6},{8,9},{9,8},{10,11... | collective-permute-start | bytes 1544 | tf_op jit(solution)/shard_map/ppermute | solution.py:271
  62.8 3.9 %collective-permute-start.16 = (f32[2,64]{1,0:T(2,128)S(1)}, f32[2,64]{1,0:T(2,128)S(1)}, u32[]{:S(2)}, u32[]{:S(2)}) collective-permute-start(f32[2,64]{1,0:T(2,128)S(1)} %add.34), channel_id=1, source_target_pairs={{0,2},{1,3},{2,0},{3,1},{4,6},{5,7},{6,4},{7,5},{8,10},{9,11},{10,... | collective-permute-start | bytes 1544 | tf_op jit(solution)/shard_map/ppermute | solution.py:272

commit v3 on v2

--- a/solution.py
+++ b/solution.py
@@ -140,8 +140,8 @@
     diag = jnp.where(eye, fac, 0.0)
     trace_l = jnp.sum(jnp.where(left, diag, 0.0))
     trace_r = jnp.sum(jnp.where(left, 0.0, diag))
-    damp = jnp.where(left, trace_l, trace_r) * (DAMP / rank)
-    mat = fac + jnp.where(eye, damp, 0.0)
+    shrink = 1.0 / (jnp.where(left, trace_l, trace_r) * (1.0 / rank))
+    mat = fac * shrink + jnp.where(eye, DAMP, 0.0)
     def column(source, k):
         return jnp.where(left, source[:, k : k + 1], source[:, rank + k : rank + k + 1])
 
@@ -168,6 +168,7 @@
             following.append(jnp.where(row == k, m0, jnp.where(row == k + 1, m1, rest)))
         if following:
             c0, c1 = following
+    mat = mat * shrink
     inv_in = mat[:, :rank]
     inv_out = mat[:, rank:]
     left_solved = jnp.dot(inv_in, grad_ref[...], precision=HIGH, preferred_element_type=jnp.float32)
@@ -256,7 +257,7 @@
     near = project(1, args, after=cross)
     near_in = lax.ppermute(near, "mp", xor_pairs(members, 1))
     mine = project(0, args, after=near)
-    gathered = widen(gathered, 0, far)
+    gathered = widen(gathered, 0, cross)
     gathered = widen(gathered, 1, near)
     gathered = widen(gathered, 2, mine)
     fac, grads = moments(clips, mine + cross_in, near_in)

time: 67.5 us -> 67.5 us (level)
  no operation moved by 1% of the time
where the time goes in v3:
time: 67.5 us; the launch traced here: 67.3 us
  starting transfers between devices  36.6 us (54%)
  Pallas kernels  16 us (24%)
  waiting for transfers between devices  13.7 us (20%)
  other arithmetic  0.8 us (1%)
    pallas_call x4, Pallas kernels, project(): pl.pallas_call(functools.partial(project_kernel, offset, query is not Non...  12 us
    ppermute x5, starting transfers between devices, local(): fac = fac + lax.ppermute(fac, 'dp', xor_pairs(groups, bit))  9.82 us
    ppermute x6, starting transfers between devices, widen(): return jnp.concatenate([blocks, lax.ppermute(blocks, 'dp', pairs)])  9.49 us
    ppermute x5, waiting for transfers between devices, local(): fac = fac + lax.ppermute(fac, 'dp', xor_pairs(groups, bit))  8.58 us
    ppermute x1, starting transfers between devices, local(): out = out + lax.ppermute(out, 'mp', xor_pairs(members, 1))  7.78 us
    ppermute x1, starting transfers between devices, local(): far_in = lax.ppermute(far, 'mp', xor_pairs(members, 1))  3.33 us
    ppermute x1, starting transfers between devices, local(): cross_in = lax.ppermute(cross, 'mp', xor_pairs(members, 2))  2.92 us
    pallas_call x1, Pallas kernels, solve(): pl.pallas_call(functools.partial(solve_kernel, clips, total), in_specs=[v...  2.82 us
  transfers between devices with their start and end apart: 17, of which 9 were waited for; matrix products, arithmetic and copies ran while one was open for 0% of the time, Pallas kernels for 17%

profile of v3, /device:TPU:1, one launch (start us, length us, event | category | flops | bytes accessed | tf_op | source)
XLA Modules:
  0.0 67.3 jit_solution(676386146927604175)
XLA Ops:
  0.0 3.5 %project.4 = (f32[512,128]{1,0:T(8,128)}, f32[1,32,128]{2,1,0:T(8,128)S(1)}) custom-call(bf16[4,2,256,512]{3,2,1,0:T(8,128)(2,1)} %x_hbm.7, bf16[4,2,256,2048]{3,2,1,0:T(8,128)(2,1)} %g_hbm.7, bf16[4,64,512]{2,1,0:T(8,128)(2,1)} %pi_hbm.4, bf16[4,64,2048]{2,1,0:T(8,128)(2,1)} %po_hbm.7, f32[4,1,64,64]{3,2,1,0:T(8,128)} %rest_0_.1), custom_call_target="tpu_custom_call" | custom-call | flops 167772160 | bytes 2883584 | tf_op jit(solution)/shard_map/project/pallas_call | solution.py:85
  3.5 3.3 %collective-permute-start = (f32[512,128]{1,0:T(8,128)}, f32[512,128]{1,0:T(8,128)S(1)}, u32[]{:S(2)}, u32[]{:S(2)}) collective-permute-start(f32[512,128]{1,0:T(8,128)} %get-tuple-element.18), channel_id=1, source_target_pairs={{0,1},{1,0},{2,3},{3,2},{4,5},{5,4},{6,7},{7,6},{8,9},{9,8},{10,11... | collective-permute-start | bytes 786440 | tf_op jit(solution)/shard_map/ppermute | solution.py:254
  6.9 2.8 %project.5 = f32[512,128]{1,0:T(8,128)S(1)} custom-call(bf16[4,2,256,512]{3,2,1,0:T(8,128)(2,1)} %x_hbm.7, bf16[4,2,256,2048]{3,2,1,0:T(8,128)(2,1)} %g_hbm.7, bf16[4,64,512]{2,1,0:T(8,128)(2,1)} %pi_hbm.4, bf16[4,64,2048]{2,1,0:T(8,128)(2,1)} %po_hbm.7), custom_call_target="tpu_custom_call" | custom-call | flops 167772160 | bytes 2883584 | tf_op jit(solution)/shard_map/project/pallas_call | solution.py:85
  9.7 0.0 collective-permute-done
  9.7 1.3 %collective-permute-start.9 = (f32[1,32,128]{2,1,0:T(8,128)S(1)}, f32[1,32,128]{2,1,0:T(8,128)S(1)}, u32[]{:S(2)}, u32[]{:S(2)}) collective-permute-start(f32[1,32,128]{2,1,0:T(8,128)S(1)} %get-tuple-element.25), channel_id=1, source_target_pairs={{0,32},{4,36},{8,40},{12,44},{16,48},{20,52},{24,56},{28,60},{32,0... | collective-permute-start | bytes 49160 | tf_op jit(solution)/shard_map/ppermute | solution.py:250
  11.1 2.9 %collective-permute-start.1 = (f32[512,128]{1,0:T(8,128)S(1)}, f32[512,128]{1,0:T(8,128)S(1)}, u32[]{:S(2)}, u32[]{:S(2)}) collective-permute-start(f32[512,128]{1,0:T(8,128)S(1)} %add.27), channel_id=1, source_target_pairs={{0,2},{1,3},{2,0},{3,1},{4,6},{5,7},{6,4},{7,5},{8,10},{9,11},{10,... | collective-permute-start | bytes 786440 | tf_op jit(solution)/shard_map/ppermute | solution.py:256
  14.0 2.8 %project.6 = f32[512,128]{1,0:T(8,128)S(1)} custom-call(bf16[4,2,256,512]{3,2,1,0:T(8,128)(2,1)} %x_hbm.7, bf16[4,2,256,2048]{3,2,1,0:T(8,128)(2,1)} %g_hbm.7, bf16[4,64,512]{2,1,0:T(8,128)(2,1)} %pi_hbm.4, bf16[4,64,2048]{2,1,0:T(8,128)(2,1)} %po_hbm.7), custom_call_target="tpu_custom_call" | custom-call | flops 167772160 | bytes 2883584 | tf_op jit(solution)/shard_map/project/pallas_call | solution.py:85
  16.8 0.7 collective-permute-start.2
  17.5 0.0 collective-permute-done.9
  17.5 1.6 %collective-permute-start.10 = (f32[2,32,128]{2,1,0:T(8,128)S(1)}, f32[2,32,128]{2,1,0:T(8,128)S(1)}, u32[]{:S(2)}, u32[]{:S(2)}) collective-permute-start(f32[2,32,128]{2,1,0:T(8,128)S(1)} %pad_maximum_fusion.5), channel_id=1, source_target_pairs={{0,16},{4,20},{8,24},{12,28},{16,0},{20,4},{24,8},{28,12},{32,48},... | collective-permute-start | bytes 98312 | tf_op jit(solution)/shard_map/ppermute | solution.py:250
  19.1 2.8 %project.7 = f32[512,128]{1,0:T(8,128)S(1)} custom-call(bf16[4,2,256,512]{3,2,1,0:T(8,128)(2,1)} %x_hbm.7, bf16[4,2,256,2048]{3,2,1,0:T(8,128)(2,1)} %g_hbm.7, bf16[4,64,512]{2,1,0:T(8,128)(2,1)} %pi_hbm.4, bf16[4,64,2048]{2,1,0:T(8,128)(2,1)} %po_hbm.7), custom_call_target="tpu_custom_call" | custom-call | flops 167772160 | bytes 2883584 | tf_op jit(solution)/shard_map/project/pallas_call | solution.py:85
  21.9 0.0 collective-permute-done.10
  22.0 3.4 %collective-permute-start.11 = (f32[4,32,128]{2,1,0:T(8,128)S(1)}, f32[4,32,128]{2,1,0:T(8,128)S(1)}, u32[]{:S(2)}, u32[]{:S(2)}) collective-permute-start(f32[4,32,128]{2,1,0:T(8,128)S(1)} %pad_maximum_fusion.4), channel_id=1, source_target_pairs={{0,96},{4,100},{8,104},{12,108},{16,112},{20,116},{24,120},{28,124... | collective-permute-start | bytes 196616 | tf_op jit(solution)/shard_map/ppermute | solution.py:250
  25.3 0.0 collective-permute-done.1
  25.4 0.0 collective-permute-done.2.b_ref
  25.4 0.4 moments.1
  25.8 1.3 %collective-permute-start.3 = (f32[64,128]{1,0:T(8,128)S(1)}, f32[64,128]{1,0:T(8,128)S(1)}, u32[]{:S(2)}, u32[]{:S(2)}) collective-permute-start(f32[64,128]{1,0:T(8,128)S(1)} %get-tuple-element.22), channel_id=1, source_target_pairs={{0,4},{4,0},{8,12},{12,8},{16,20},{20,16},{24,28},{28,24},{32,36},... | collective-permute-start | bytes 98312 | tf_op jit(solution)/shard_map/ppermute | solution.py:267
  27.1 0.2 collective-permute-done.11
  27.3 1.4 %collective-permute-done.3 = f32[64,128]{1,0:T(8,128)S(1)} collective-permute-done((f32[64,128]{1,0:T(8,128)S(1)}, f32[64,128]{1,0:T(8,128)S(1)}, u32[]{:S(2)}, u32[]{:S(2)}) %collective-permute-start.3) | collective-permute-done | bytes 32800 | tf_op jit(solution)/shard_map/ppermute | solution.py:267
  28.7 0.4 collective-permute-start.12
  29.1 2.5 %collective-permute-start.4 = (f32[64,128]{1,0:T(8,128)S(1)}, f32[64,128]{1,0:T(8,128)S(1)}, u32[]{:S(2)}, u32[]{:S(2)}) collective-permute-start(f32[64,128]{1,0:T(8,128)S(1)} %add.29), channel_id=1, source_target_pairs={{0,12},{4,8},{8,4},{12,0},{16,28},{20,24},{24,20},{28,16},{32,44},... | collective-permute-start | bytes 98312 | tf_op jit(solution)/shard_map/ppermute | solution.py:267
  31.6 1.5 %collective-permute-done.4 = f32[64,128]{1,0:T(8,128)S(1)} collective-permute-done((f32[64,128]{1,0:T(8,128)S(1)}, f32[64,128]{1,0:T(8,128)S(1)}, u32[]{:S(2)}, u32[]{:S(2)}) %collective-permute-start.4) | collective-permute-done | bytes 32800 | tf_op jit(solution)/shard_map/ppermute | solution.py:267
  33.1 0.0 collective-permute-done.12
  33.1 0.7 %collective-permute-start.13 = (f32[16,32,128]{2,1,0:T(8,128)S(1)}, f32[16,32,128]{2,1,0:T(8,128)S(1)}, u32[]{:S(2)}, u32[]{:S(2)}) collective-permute-start(f32[16,32,128]{2,1,0:T(8,128)S(1)} %pad_maximum_fusion.2), channel_id=1, source_target_pairs={{0,4},{4,0},{8,12},{12,8},{16,20},{20,16},{24,28},{28,24},{32,36},... | collective-permute-start | bytes 786440 | tf_op jit(solution)/shard_map/ppermute | solution.py:250
  33.8 1.0 %collective-permute-start.5 = (f32[64,128]{1,0:T(8,128)S(1)}, f32[64,128]{1,0:T(8,128)S(1)}, u32[]{:S(2)}, u32[]{:S(2)}) collective-permute-start(f32[64,128]{1,0:T(8,128)S(1)} %add.30), channel_id=1, source_target_pairs={{0,16},{4,20},{8,24},{12,28},{16,0},{20,4},{24,8},{28,12},{32,48},... | collective-permute-start | bytes 98312 | tf_op jit(solution)/shard_map/ppermute | solution.py:267
  34.9 1.7 %collective-permute-done.5 = f32[64,128]{1,0:T(8,128)S(1)} collective-permute-done((f32[64,128]{1,0:T(8,128)S(1)}, f32[64,128]{1,0:T(8,128)S(1)}, u32[]{:S(2)}, u32[]{:S(2)}) %collective-permute-start.5) | collective-permute-done | bytes 32800 | tf_op jit(solution)/shard_map/ppermute | solution.py:267
  36.6 3.9 %collective-permute-start.6 = (f32[64,128]{1,0:T(8,128)S(1)}, f32[64,128]{1,0:T(8,128)S(1)}, u32[]{:S(2)}, u32[]{:S(2)}) collective-permute-start(f32[64,128]{1,0:T(8,128)S(1)} %add.31), channel_id=1, source_target_pairs={{0,96},{4,100},{8,104},{12,108},{16,112},{20,116},{24,120},{28,124... | collective-permute-start | bytes 98312 | tf_op jit(solution)/shard_map/ppermute | solution.py:267
  40.5 1.4 %collective-permute-done.6 = f32[64,128]{1,0:T(8,128)S(1)} collective-permute-done((f32[64,128]{1,0:T(8,128)S(1)}, f32[64,128]{1,0:T(8,128)S(1)}, u32[]{:S(2)}, u32[]{:S(2)}) %collective-permute-start.6) | collective-permute-done | bytes 32800 | tf_op jit(solution)/shard_map/ppermute | solution.py:267
  41.9 0.0 collective-permute-done.13
  42.0 2.0 %collective-permute-start.14 = (f32[32,32,128]{2,1,0:T(8,128)S(1)}, f32[32,32,128]{2,1,0:T(8,128)S(1)}, u32[]{:S(2)}, u32[]{:S(2)}) collective-permute-start(f32[32,32,128]{2,1,0:T(8,128)S(1)} %pad_maximum_fusion.1), channel_id=1, source_target_pairs={{0,12},{4,8},{8,4},{12,0},{16,28},{20,24},{24,20},{28,16},{32,44},... | collective-permute-start | bytes 1572872 | tf_op jit(solution)/shard_map/ppermute | solution.py:250
  44.0 1.1 %collective-permute-start.7 = (f32[64,128]{1,0:T(8,128)S(1)}, f32[64,128]{1,0:T(8,128)S(1)}, u32[]{:S(2)}, u32[]{:S(2)}) collective-permute-start(f32[64,128]{1,0:T(8,128)S(1)} %add.32), channel_id=1, source_target_pairs={{0,32},{4,36},{8,40},{12,44},{16,48},{20,52},{24,56},{28,60},{32,0... | collective-permute-start | bytes 98312 | tf_op jit(solution)/shard_map/ppermute | solution.py:267
  45.1 2.6 %collective-permute-done.7 = f32[64,128]{1,0:T(8,128)S(1)} collective-permute-done((f32[64,128]{1,0:T(8,128)S(1)}, f32[64,128]{1,0:T(8,128)S(1)}, u32[]{:S(2)}, u32[]{:S(2)}) %collective-permute-start.7) | collective-permute-done | bytes 32800 | tf_op jit(solution)/shard_map/ppermute | solution.py:267
  47.7 1.1 %collective-permute-start.8 = (f32[64,128]{1,0:T(8,128)S(1)}, f32[64,128]{1,0:T(8,128)S(1)}, u32[]{:S(2)}, u32[]{:S(2)}) collective-permute-start(f32[64,128]{1,0:T(8,128)S(1)} %add.33.fa_ref), channel_id=1, source_target_pairs={{0,128},{4,132},{8,136},{12,140},{16,144},{20,148},{24,152},{28,15... | collective-permute-start | bytes 98312 | tf_op jit(solution)/shard_map/ppermute | solution.py:268
  48.7 1.7 %collective-permute-done.8.fb_ref = f32[64,128]{1,0:T(8,128)S(1)} collective-permute-done((f32[64,128]{1,0:T(8,128)S(1)}, f32[64,128]{1,0:T(8,128)S(1)}, u32[]{:S(2)}, u32[]{:S(2)}) %collective-permute-start.8) | collective-permute-done | bytes 32800 | tf_op jit(solution)/shard_map/ppermute | solution.py:268
  50.4 2.8 %solve.1.solved_ref = f32[2,32,128]{2,1,0:T(8,128)S(1)} custom-call(f32[64,128]{1,0:T(8,128)S(1)} %add.33.fa_ref, f32[64,128]{1,0:T(8,128)S(1)} %collective-permute-done.8.fb_ref, f32[64,128]{1,0:T(8,128)S(1)} %get-tuple-element.23.grad_ref), custom_call_target="tpu_custom_call" | custom-call | bytes 8000000 | tf_op jit(solution)/shard_map/solve/pallas_call | solution.py:187
  53.3 0.0 collective-permute-done.14
  53.3 0.1 pad_maximum_fusion.q_ref
  53.3 0.8 %contract.1 = f32[2,64]{1,0:T(2,128)S(1)} custom-call(f32[2,32,128]{2,1,0:T(8,128)S(1)} %solve.1.solved_ref, f32[64,32,128]{2,1,0:T(8,128)S(1)} %pad_maximum_fusion.q_ref), custom_call_target="tpu_custom_call" | custom-call | tf_op jit(solution)/shard_map/contract/pallas_call | solution.py:230
  54.2 7.8 %collective-permute-start.15 = (f32[2,64]{1,0:T(2,128)S(1)}, f32[2,64]{1,0:T(2,128)S(1)}, u32[]{:S(2)}, u32[]{:S(2)}) collective-permute-start(f32[2,64]{1,0:T(2,128)S(1)} %contract.1), channel_id=1, source_target_pairs={{0,1},{1,0},{2,3},{3,2},{4,5},{5,4},{6,7},{7,6},{8,9},{9,8},{10,11... | collective-permute-start | bytes 1544 | tf_op jit(solution)/shard_map/ppermute | solution.py:272
  62.0 0.8 %collective-permute-done.15 = f32[2,64]{1,0:T(2,128)S(1)} collective-permute-done((f32[2,64]{1,0:T(2,128)S(1)}, f32[2,64]{1,0:T(2,128)S(1)}, u32[]{:S(2)}, u32[]{:S(2)}) %collective-permute-start.15) | collective-permute-done | bytes 544 | tf_op jit(solution)/shard_map/ppermute | solution.py:272
  62.8 1.6 %collective-permute-start.16 = (f32[2,64]{1,0:T(2,128)S(1)}, f32[2,64]{1,0:T(2,128)S(1)}, u32[]{:S(2)}, u32[]{:S(2)}) collective-permute-start(f32[2,64]{1,0:T(2,128)S(1)} %add.34), channel_id=1, source_target_pairs={{0,2},{1,3},{2,0},{3,1},{4,6},{5,7},{6,4},{7,5},{8,10},{9,11},{10,... | collective-permute-start | bytes 1544 | tf_op jit(solution)/shard_map/ppermute | solution.py:273
  64.3 2.4 %collective-permute-done.16 = f32[2,64]{1,0:T(2,128)S(1)} collective-permute-done((f32[2,64]{1,0:T(2,128)S(1)}, f32[2,64]{1,0:T(2,128)S(1)}, u32[]{:S(2)}, u32[]{:S(2)}) %collective-permute-start.16) | collective-permute-done | bytes 544 | tf_op jit(solution)/shard_map/ppermute | solution.py:273
  66.7 0.6 add.35
  (13 shorter events, 0.2 us)
Async XLA Ops:
  3.5 6.1 %collective-permute-start = (f32[512,128]{1,0:T(8,128)}, f32[512,128]{1,0:T(8,128)S(1)}, u32[]{:S(2)}, u32[]{:S(2)}) collective-permute-start(f32[512,128]{1,0:T(8,128)} %get-tuple-element.18), channel_id=1, source_target_pairs={{0,1},{1,0},{2,3},{3,2},{4,5},{5,4},{6,7},{7,6},{8,9},{9,8},{10,11... | collective-permute-start | bytes 786440 | tf_op jit(solution)/shard_map/ppermute | solution.py:254
  9.7 7.7 %collective-permute-start.9 = (f32[1,32,128]{2,1,0:T(8,128)S(1)}, f32[1,32,128]{2,1,0:T(8,128)S(1)}, u32[]{:S(2)}, u32[]{:S(2)}) collective-permute-start(f32[1,32,128]{2,1,0:T(8,128)S(1)} %get-tuple-element.25), channel_id=1, source_target_pairs={{0,32},{4,36},{8,40},{12,44},{16,48},{20,52},{24,56},{28,60},{32,0... | collective-permute-start | bytes 49160 | tf_op jit(solution)/shard_map/ppermute | solution.py:250
  11.1 14.3 %collective-permute-start.1 = (f32[512,128]{1,0:T(8,128)S(1)}, f32[512,128]{1,0:T(8,128)S(1)}, u32[]{:S(2)}, u32[]{:S(2)}) collective-permute-start(f32[512,128]{1,0:T(8,128)S(1)} %add.27), channel_id=1, source_target_pairs={{0,2},{1,3},{2,0},{3,1},{4,6},{5,7},{6,4},{7,5},{8,10},{9,11},{10,... | collective-permute-start | bytes 786440 | tf_op jit(solution)/shard_map/ppermute | solution.py:256
  16.8 8.6 %collective-permute-start.2 = (f32[512,128]{1,0:T(8,128)S(1)}, f32[512,128]{1,0:T(8,128)S(1)}, u32[]{:S(2)}, u32[]{:S(2)}) collective-permute-start(f32[512,128]{1,0:T(8,128)S(1)} %project.6), channel_id=1, source_target_pairs={{0,1},{1,0},{2,3},{3,2},{4,5},{5,4},{6,7},{7,6},{8,9},{9,8},{10,11... | collective-permute-start | bytes 786440 | tf_op jit(solution)/shard_map/ppermute | solution.py:258
  17.5 4.5 %collective-permute-start.10 = (f32[2,32,128]{2,1,0:T(8,128)S(1)}, f32[2,32,128]{2,1,0:T(8,128)S(1)}, u32[]{:S(2)}, u32[]{:S(2)}) collective-permute-start(f32[2,32,128]{2,1,0:T(8,128)S(1)} %pad_maximum_fusion.5), channel_id=1, source_target_pairs={{0,16},{4,20},{8,24},{12,28},{16,0},{20,4},{24,8},{28,12},{32,48},... | collective-permute-start | bytes 98312 | tf_op jit(solution)/shard_map/ppermute | solution.py:250
  22.0 5.3 %collective-permute-start.11 = (f32[4,32,128]{2,1,0:T(8,128)S(1)}, f32[4,32,128]{2,1,0:T(8,128)S(1)}, u32[]{:S(2)}, u32[]{:S(2)}) collective-permute-start(f32[4,32,128]{2,1,0:T(8,128)S(1)} %pad_maximum_fusion.4), channel_id=1, source_target_pairs={{0,96},{4,100},{8,104},{12,108},{16,112},{20,116},{24,120},{28,124... | collective-permute-start | bytes 196616 | tf_op jit(solution)/shard_map/ppermute | solution.py:250
  25.8 2.9 %collective-permute-start.3 = (f32[64,128]{1,0:T(8,128)S(1)}, f32[64,128]{1,0:T(8,128)S(1)}, u32[]{:S(2)}, u32[]{:S(2)}) collective-permute-start(f32[64,128]{1,0:T(8,128)S(1)} %get-tuple-element.22), channel_id=1, source_target_pairs={{0,4},{4,0},{8,12},{12,8},{16,20},{20,16},{24,28},{28,24},{32,36},... | collective-permute-start | bytes 98312 | tf_op jit(solution)/shard_map/ppermute | solution.py:267
  28.7 4.4 %collective-permute-start.12 = (f32[8,32,128]{2,1,0:T(8,128)S(1)}, f32[8,32,128]{2,1,0:T(8,128)S(1)}, u32[]{:S(2)}, u32[]{:S(2)}) collective-permute-start(f32[8,32,128]{2,1,0:T(8,128)S(1)} %pad_maximum_fusion.3), channel_id=1, source_target_pairs={{0,128},{4,132},{8,136},{12,140},{16,144},{20,148},{24,152},{28,15... | collective-permute-start | bytes 393224 | tf_op jit(solution)/shard_map/ppermute | solution.py:250
  29.1 4.0 %collective-permute-start.4 = (f32[64,128]{1,0:T(8,128)S(1)}, f32[64,128]{1,0:T(8,128)S(1)}, u32[]{:S(2)}, u32[]{:S(2)}) collective-permute-start(f32[64,128]{1,0:T(8,128)S(1)} %add.29), channel_id=1, source_target_pairs={{0,12},{4,8},{8,4},{12,0},{16,28},{20,24},{24,20},{28,16},{32,44},... | collective-permute-start | bytes 98312 | tf_op jit(solution)/shard_map/ppermute | solution.py:267
  33.1 8.8 %collective-permute-start.13 = (f32[16,32,128]{2,1,0:T(8,128)S(1)}, f32[16,32,128]{2,1,0:T(8,128)S(1)}, u32[]{:S(2)}, u32[]{:S(2)}) collective-permute-start(f32[16,32,128]{2,1,0:T(8,128)S(1)} %pad_maximum_fusion.2), channel_id=1, source_target_pairs={{0,4},{4,0},{8,12},{12,8},{16,20},{20,16},{24,28},{28,24},{32,36},... | collective-permute-start | bytes 786440 | tf_op jit(solution)/shard_map/ppermute | solution.py:250
  33.8 2.8 %collective-permute-start.5 = (f32[64,128]{1,0:T(8,128)S(1)}, f32[64,128]{1,0:T(8,128)S(1)}, u32[]{:S(2)}, u32[]{:S(2)}) collective-permute-start(f32[64,128]{1,0:T(8,128)S(1)} %add.30), channel_id=1, source_target_pairs={{0,16},{4,20},{8,24},{12,28},{16,0},{20,4},{24,8},{28,12},{32,48},... | collective-permute-start | bytes 98312 | tf_op jit(solution)/shard_map/ppermute | solution.py:267
  36.6 5.3 %collective-permute-start.6 = (f32[64,128]{1,0:T(8,128)S(1)}, f32[64,128]{1,0:T(8,128)S(1)}, u32[]{:S(2)}, u32[]{:S(2)}) collective-permute-start(f32[64,128]{1,0:T(8,128)S(1)} %add.31), channel_id=1, source_target_pairs={{0,96},{4,100},{8,104},{12,108},{16,112},{20,116},{24,120},{28,124... | collective-permute-start | bytes 98312 | tf_op jit(solution)/shard_map/ppermute | solution.py:267
  42.0 11.3 %collective-permute-start.14 = (f32[32,32,128]{2,1,0:T(8,128)S(1)}, f32[32,32,128]{2,1,0:T(8,128)S(1)}, u32[]{:S(2)}, u32[]{:S(2)}) collective-permute-start(f32[32,32,128]{2,1,0:T(8,128)S(1)} %pad_maximum_fusion.1), channel_id=1, source_target_pairs={{0,12},{4,8},{8,4},{12,0},{16,28},{20,24},{24,20},{28,16},{32,44},... | collective-permute-start | bytes 1572872 | tf_op jit(solution)/shard_map/ppermute | solution.py:250
  44.0 3.7 %collective-permute-start.7 = (f32[64,128]{1,0:T(8,128)S(1)}, f32[64,128]{1,0:T(8,128)S(1)}, u32[]{:S(2)}, u32[]{:S(2)}) collective-permute-start(f32[64,128]{1,0:T(8,128)S(1)} %add.32), channel_id=1, source_target_pairs={{0,32},{4,36},{8,40},{12,44},{16,48},{20,52},{24,56},{28,60},{32,0... | collective-permute-start | bytes 98312 | tf_op jit(solution)/shard_map/ppermute | solution.py:267
  47.7 2.8 %collective-permute-start.8 = (f32[64,128]{1,0:T(8,128)S(1)}, f32[64,128]{1,0:T(8,128)S(1)}, u32[]{:S(2)}, u32[]{:S(2)}) collective-permute-start(f32[64,128]{1,0:T(8,128)S(1)} %add.33.fa_ref), channel_id=1, source_target_pairs={{0,128},{4,132},{8,136},{12,140},{16,144},{20,148},{24,152},{28,15... | collective-permute-start | bytes 98312 | tf_op jit(solution)/shard_map/ppermute | solution.py:268
  54.2 8.6 %collective-permute-start.15 = (f32[2,64]{1,0:T(2,128)S(1)}, f32[2,64]{1,0:T(2,128)S(1)}, u32[]{:S(2)}, u32[]{:S(2)}) collective-permute-start(f32[2,64]{1,0:T(2,128)S(1)} %contract.1), channel_id=1, source_target_pairs={{0,1},{1,0},{2,3},{3,2},{4,5},{5,4},{6,7},{7,6},{8,9},{9,8},{10,11... | collective-permute-start | bytes 1544 | tf_op jit(solution)/shard_map/ppermute | solution.py:272
  62.8 3.9 %collective-permute-start.16 = (f32[2,64]{1,0:T(2,128)S(1)}, f32[2,64]{1,0:T(2,128)S(1)}, u32[]{:S(2)}, u32[]{:S(2)}) collective-permute-start(f32[2,64]{1,0:T(2,128)S(1)} %add.34), channel_id=1, source_target_pairs={{0,2},{1,3},{2,0},{3,1},{4,6},{5,7},{6,4},{7,5},{8,10},{9,11},{10,... | collective-permute-start | bytes 1544 | tf_op jit(solution)/shard_map/ppermute | solution.py:273

commit v4 on v3

--- a/solution.py
+++ b/solution.py
@@ -8,7 +8,6 @@
 from jax.sharding import PartitionSpec as P
 
 DAMP = 0.1
-QUERY_VMEM = 56426496
 VMEM = 53 * 2**20 + 2**19
 QUERY_BITS = (8, 4, 24, 32, 1, 3)
 QUERY_AT = {1: 3, 2: 4, 4: 5}
@@ -88,7 +87,7 @@
         out_specs=out_specs,
         out_shape=out_shape,
         scratch_shapes=scratch,
-        compiler_params=pltpu.CompilerParams(vmem_limit_bytes=VMEM if query is None else QUERY_VMEM),
+        compiler_params=pltpu.CompilerParams(vmem_limit_bytes=VMEM),
         cost_estimate=pl.CostEstimate(
             flops=rows * (width + hidden) * rank * 2,
             bytes_accessed=rows * (width + hidden) * 2 + rows * rank * 8,
@@ -250,9 +249,10 @@
         return jnp.concatenate([blocks, lax.ppermute(blocks, "dp", pairs)])
 
     args = (activations, out_grads, proj_in, proj_out)
-    far, gathered = project(3, args, query=query_grads)
+    far = project(3, args)
     far_in = lax.ppermute(far, "mp", xor_pairs(members, 1))
-    cross = project(2, args, after=far) + far_in
+    cross, gathered = project(2, args, query=query_grads, after=far)
+    cross = cross + far_in
     cross_in = lax.ppermute(cross, "mp", xor_pairs(members, 2))
     near = project(1, args, after=cross)
     near_in = lax.ppermute(near, "mp", xor_pairs(members, 1))

time: 67.5 us -> 66.9 us (level)
  transfers between devices with their start and end apart: 17 -> 17, of which waited for: 9 -> 9; matrix products, arithmetic and copies ran while one was open for 0% -> 0% of each run, Pallas kernels for 17% -> 18%
where the time goes in v4:
time: 66.9 us; the launch traced here: 66.7 us
  starting transfers between devices  36.7 us (55%)
  Pallas kernels  15.4 us (23%)
  waiting for transfers between devices  13.7 us (20%)
  other arithmetic  0.8 us (1%)
    pallas_call x4, Pallas kernels, project(): pl.pallas_call(functools.partial(project_kernel, offset, query is not Non...  11.4 us
    ppermute x5, starting transfers between devices, local(): fac = fac + lax.ppermute(fac, 'dp', xor_pairs(groups, bit))  9.8 us
    ppermute x6, starting transfers between devices, widen(): return jnp.concatenate([blocks, lax.ppermute(blocks, 'dp', pairs)])  9.5 us
    ppermute x5, waiting for transfers between devices, local(): fac = fac + lax.ppermute(fac, 'dp', xor_pairs(groups, bit))  8.59 us
    ppermute x1, starting transfers between devices, local(): out = out + lax.ppermute(out, 'mp', xor_pairs(members, 1))  7.78 us
    ppermute x1, starting transfers between devices, local(): far_in = lax.ppermute(far, 'mp', xor_pairs(members, 1))  3.33 us
    ppermute x1, starting transfers between devices, local(): cross_in = lax.ppermute(cross, 'mp', xor_pairs(members, 2))  2.92 us
    pallas_call x1, Pallas kernels, solve(): pl.pallas_call(functools.partial(solve_kernel, clips, total), in_specs=[v...  2.82 us
  transfers between devices with their start and end apart: 17, of which 9 were waited for; matrix products, arithmetic and copies ran while one was open for 0% of the time, Pallas kernels for 18%

profile of v4, /device:TPU:1, one launch (start us, length us, event | category | flops | bytes accessed | tf_op | source)
XLA Modules:
  0.0 66.7 jit_solution(7209811052815955132)
XLA Ops:
  0.0 0.0 copy-start
  0.0 2.8 %project.4 = f32[512,128]{1,0:T(8,128)S(1)} custom-call(bf16[4,2,256,512]{3,2,1,0:T(8,128)(2,1)} %x_hbm.7, bf16[4,2,256,2048]{3,2,1,0:T(8,128)(2,1)} %g_hbm.7, bf16[4,64,512]{2,1,0:T(8,128)(2,1)} %pi_hbm.4, bf16[4,64,2048]{2,1,0:T(8,128)(2,1)} %po_hbm.7), custom_call_target="tpu_custom_call" | custom-call | flops 167772160 | bytes 2883584 | tf_op jit(solution)/shard_map/project/pallas_call | solution.py:84
  2.8 3.3 %collective-permute-start = (f32[512,128]{1,0:T(8,128)S(1)}, f32[512,128]{1,0:T(8,128)S(1)}, u32[]{:S(2)}, u32[]{:S(2)}) collective-permute-start(f32[512,128]{1,0:T(8,128)S(1)} %project.4), channel_id=1, source_target_pairs={{0,1},{1,0},{2,3},{3,2},{4,5},{5,4},{6,7},{7,6},{8,9},{9,8},{10,11... | collective-permute-start | bytes 786440 | tf_op jit(solution)/shard_map/ppermute | solution.py:253
  6.2 0.0 copy-done
  6.2 2.9 %project.5 = (f32[512,128]{1,0:T(8,128)S(1)}, f32[1,32,128]{2,1,0:T(8,128)S(1)}) custom-call(bf16[4,2,256,512]{3,2,1,0:T(8,128)(2,1)} %x_hbm.7, bf16[4,2,256,2048]{3,2,1,0:T(8,128)(2,1)} %g_hbm.7, bf16[4,64,512]{2,1,0:T(8,128)(2,1)} %pi_hbm.4, bf16[4,64,2048]{2,1,0:T(8,128)(2,1)} %po_hbm.7, f32[4,1,64,64]{3,2,1,0:T(8,128)S(1)} %copy-done), custom_call_target="tpu_custom_call" | custom-call | flops 167772160 | bytes 2883584 | tf_op jit(solution)/shard_map/project/pallas_call | solution.py:84
  9.1 0.0 collective-permute-done
  9.1 1.3 %collective-permute-start.9 = (f32[1,32,128]{2,1,0:T(8,128)S(1)}, f32[1,32,128]{2,1,0:T(8,128)S(1)}, u32[]{:S(2)}, u32[]{:S(2)}) collective-permute-start(f32[1,32,128]{2,1,0:T(8,128)S(1)} %get-tuple-element.25), channel_id=1, source_target_pairs={{0,32},{4,36},{8,40},{12,44},{16,48},{20,52},{24,56},{28,60},{32,0... | collective-permute-start | bytes 49160 | tf_op jit(solution)/shard_map/ppermute | solution.py:249
  10.5 2.9 %collective-permute-start.1 = (f32[512,128]{1,0:T(8,128)S(1)}, f32[512,128]{1,0:T(8,128)S(1)}, u32[]{:S(2)}, u32[]{:S(2)}) collective-permute-start(f32[512,128]{1,0:T(8,128)S(1)} %add.27), channel_id=1, source_target_pairs={{0,2},{1,3},{2,0},{3,1},{4,6},{5,7},{6,4},{7,5},{8,10},{9,11},{10,... | collective-permute-start | bytes 786440 | tf_op jit(solution)/shard_map/ppermute | solution.py:256
  13.4 2.8 %project.6 = f32[512,128]{1,0:T(8,128)S(1)} custom-call(bf16[4,2,256,512]{3,2,1,0:T(8,128)(2,1)} %x_hbm.7, bf16[4,2,256,2048]{3,2,1,0:T(8,128)(2,1)} %g_hbm.7, bf16[4,64,512]{2,1,0:T(8,128)(2,1)} %pi_hbm.4, bf16[4,64,2048]{2,1,0:T(8,128)(2,1)} %po_hbm.7), custom_call_target="tpu_custom_call" | custom-call | flops 167772160 | bytes 2883584 | tf_op jit(solution)/shard_map/project/pallas_call | solution.py:84
  16.2 0.7 %collective-permute-start.2 = (f32[512,128]{1,0:T(8,128)S(1)}, f32[512,128]{1,0:T(8,128)S(1)}, u32[]{:S(2)}, u32[]{:S(2)}) collective-permute-start(f32[512,128]{1,0:T(8,128)S(1)} %project.6), channel_id=1, source_target_pairs={{0,1},{1,0},{2,3},{3,2},{4,5},{5,4},{6,7},{7,6},{8,9},{9,8},{10,11... | collective-permute-start | bytes 786440 | tf_op jit(solution)/shard_map/ppermute | solution.py:258
  16.9 0.0 collective-permute-done.9
  16.9 1.6 %collective-permute-start.10 = (f32[2,32,128]{2,1,0:T(8,128)S(1)}, f32[2,32,128]{2,1,0:T(8,128)S(1)}, u32[]{:S(2)}, u32[]{:S(2)}) collective-permute-start(f32[2,32,128]{2,1,0:T(8,128)S(1)} %pad_maximum_fusion.5), channel_id=1, source_target_pairs={{0,16},{4,20},{8,24},{12,28},{16,0},{20,4},{24,8},{28,12},{32,48},... | collective-permute-start | bytes 98312 | tf_op jit(solution)/shard_map/ppermute | solution.py:249
  18.6 2.8 %project.7 = f32[512,128]{1,0:T(8,128)S(1)} custom-call(bf16[4,2,256,512]{3,2,1,0:T(8,128)(2,1)} %x_hbm.7, bf16[4,2,256,2048]{3,2,1,0:T(8,128)(2,1)} %g_hbm.7, bf16[4,64,512]{2,1,0:T(8,128)(2,1)} %pi_hbm.4, bf16[4,64,2048]{2,1,0:T(8,128)(2,1)} %po_hbm.7), custom_call_target="tpu_custom_call" | custom-call | flops 167772160 | bytes 2883584 | tf_op jit(solution)/shard_map/project/pallas_call | solution.py:84
  21.4 0.0 collective-permute-done.10
  21.4 3.4 %collective-permute-start.11 = (f32[4,32,128]{2,1,0:T(8,128)S(1)}, f32[4,32,128]{2,1,0:T(8,128)S(1)}, u32[]{:S(2)}, u32[]{:S(2)}) collective-permute-start(f32[4,32,128]{2,1,0:T(8,128)S(1)} %pad_maximum_fusion.4), channel_id=1, source_target_pairs={{0,96},{4,100},{8,104},{12,108},{16,112},{20,116},{24,120},{28,124... | collective-permute-start | bytes 196616 | tf_op jit(solution)/shard_map/ppermute | solution.py:249
  24.8 0.0 collective-permute-done.1
  24.8 0.0 collective-permute-done.2.b_ref
  24.8 0.4 moments.1
  25.3 1.3 %collective-permute-start.3 = (f32[64,128]{1,0:T(8,128)S(1)}, f32[64,128]{1,0:T(8,128)S(1)}, u32[]{:S(2)}, u32[]{:S(2)}) collective-permute-start(f32[64,128]{1,0:T(8,128)S(1)} %get-tuple-element.22), channel_id=1, source_target_pairs={{0,4},{4,0},{8,12},{12,8},{16,20},{20,16},{24,28},{28,24},{32,36},... | collective-permute-start | bytes 98312 | tf_op jit(solution)/shard_map/ppermute | solution.py:267
  26.6 0.2 collective-permute-done.11
  26.8 1.4 %collective-permute-done.3 = f32[64,128]{1,0:T(8,128)S(1)} collective-permute-done((f32[64,128]{1,0:T(8,128)S(1)}, f32[64,128]{1,0:T(8,128)S(1)}, u32[]{:S(2)}, u32[]{:S(2)}) %collective-permute-start.3) | collective-permute-done | bytes 32800 | tf_op jit(solution)/shard_map/ppermute | solution.py:267
  28.1 0.4 collective-permute-start.12
  28.5 2.5 %collective-permute-start.4 = (f32[64,128]{1,0:T(8,128)S(1)}, f32[64,128]{1,0:T(8,128)S(1)}, u32[]{:S(2)}, u32[]{:S(2)}) collective-permute-start(f32[64,128]{1,0:T(8,128)S(1)} %add.29), channel_id=1, source_target_pairs={{0,12},{4,8},{8,4},{12,0},{16,28},{20,24},{24,20},{28,16},{32,44},... | collective-permute-start | bytes 98312 | tf_op jit(solution)/shard_map/ppermute | solution.py:267
  31.0 1.5 %collective-permute-done.4 = f32[64,128]{1,0:T(8,128)S(1)} collective-permute-done((f32[64,128]{1,0:T(8,128)S(1)}, f32[64,128]{1,0:T(8,128)S(1)}, u32[]{:S(2)}, u32[]{:S(2)}) %collective-permute-start.4) | collective-permute-done | bytes 32800 | tf_op jit(solution)/shard_map/ppermute | solution.py:267
  32.5 0.0 collective-permute-done.12
  32.5 0.7 %collective-permute-start.13 = (f32[16,32,128]{2,1,0:T(8,128)S(1)}, f32[16,32,128]{2,1,0:T(8,128)S(1)}, u32[]{:S(2)}, u32[]{:S(2)}) collective-permute-start(f32[16,32,128]{2,1,0:T(8,128)S(1)} %pad_maximum_fusion.2), channel_id=1, source_target_pairs={{0,4},{4,0},{8,12},{12,8},{16,20},{20,16},{24,28},{28,24},{32,36},... | collective-permute-start | bytes 786440 | tf_op jit(solution)/shard_map/ppermute | solution.py:249
  33.3 1.0 %collective-permute-start.5 = (f32[64,128]{1,0:T(8,128)S(1)}, f32[64,128]{1,0:T(8,128)S(1)}, u32[]{:S(2)}, u32[]{:S(2)}) collective-permute-start(f32[64,128]{1,0:T(8,128)S(1)} %add.30), channel_id=1, source_target_pairs={{0,16},{4,20},{8,24},{12,28},{16,0},{20,4},{24,8},{28,12},{32,48},... | collective-permute-start | bytes 98312 | tf_op jit(solution)/shard_map/ppermute | solution.py:267
  34.3 1.7 %collective-permute-done.5 = f32[64,128]{1,0:T(8,128)S(1)} collective-permute-done((f32[64,128]{1,0:T(8,128)S(1)}, f32[64,128]{1,0:T(8,128)S(1)}, u32[]{:S(2)}, u32[]{:S(2)}) %collective-permute-start.5) | collective-permute-done | bytes 32800 | tf_op jit(solution)/shard_map/ppermute | solution.py:267
  36.0 3.9 %collective-permute-start.6 = (f32[64,128]{1,0:T(8,128)S(1)}, f32[64,128]{1,0:T(8,128)S(1)}, u32[]{:S(2)}, u32[]{:S(2)}) collective-permute-start(f32[64,128]{1,0:T(8,128)S(1)} %add.31), channel_id=1, source_target_pairs={{0,96},{4,100},{8,104},{12,108},{16,112},{20,116},{24,120},{28,124... | collective-permute-start | bytes 98312 | tf_op jit(solution)/shard_map/ppermute | solution.py:267
  39.9 1.4 %collective-permute-done.6 = f32[64,128]{1,0:T(8,128)S(1)} collective-permute-done((f32[64,128]{1,0:T(8,128)S(1)}, f32[64,128]{1,0:T(8,128)S(1)}, u32[]{:S(2)}, u32[]{:S(2)}) %collective-permute-start.6) | collective-permute-done | bytes 32800 | tf_op jit(solution)/shard_map/ppermute | solution.py:267
  41.4 0.0 collective-permute-done.13
  41.4 2.0 %collective-permute-start.14 = (f32[32,32,128]{2,1,0:T(8,128)S(1)}, f32[32,32,128]{2,1,0:T(8,128)S(1)}, u32[]{:S(2)}, u32[]{:S(2)}) collective-permute-start(f32[32,32,128]{2,1,0:T(8,128)S(1)} %pad_maximum_fusion.1), channel_id=1, source_target_pairs={{0,12},{4,8},{8,4},{12,0},{16,28},{20,24},{24,20},{28,16},{32,44},... | collective-permute-start | bytes 1572872 | tf_op jit(solution)/shard_map/ppermute | solution.py:249
  43.4 1.1 %collective-permute-start.7 = (f32[64,128]{1,0:T(8,128)S(1)}, f32[64,128]{1,0:T(8,128)S(1)}, u32[]{:S(2)}, u32[]{:S(2)}) collective-permute-start(f32[64,128]{1,0:T(8,128)S(1)} %add.32), channel_id=1, source_target_pairs={{0,32},{4,36},{8,40},{12,44},{16,48},{20,52},{24,56},{28,60},{32,0... | collective-permute-start | bytes 98312 | tf_op jit(solution)/shard_map/ppermute | solution.py:267
  44.6 2.5 %collective-permute-done.7 = f32[64,128]{1,0:T(8,128)S(1)} collective-permute-done((f32[64,128]{1,0:T(8,128)S(1)}, f32[64,128]{1,0:T(8,128)S(1)}, u32[]{:S(2)}, u32[]{:S(2)}) %collective-permute-start.7) | collective-permute-done | bytes 32800 | tf_op jit(solution)/shard_map/ppermute | solution.py:267
  47.1 1.1 %collective-permute-start.8 = (f32[64,128]{1,0:T(8,128)S(1)}, f32[64,128]{1,0:T(8,128)S(1)}, u32[]{:S(2)}, u32[]{:S(2)}) collective-permute-start(f32[64,128]{1,0:T(8,128)S(1)} %add.33.fa_ref), channel_id=1, source_target_pairs={{0,128},{4,132},{8,136},{12,140},{16,144},{20,148},{24,152},{28,15... | collective-permute-start | bytes 98312 | tf_op jit(solution)/shard_map/ppermute | solution.py:268
  48.2 1.7 %collective-permute-done.8.fb_ref = f32[64,128]{1,0:T(8,128)S(1)} collective-permute-done((f32[64,128]{1,0:T(8,128)S(1)}, f32[64,128]{1,0:T(8,128)S(1)}, u32[]{:S(2)}, u32[]{:S(2)}) %collective-permute-start.8) | collective-permute-done | bytes 32800 | tf_op jit(solution)/shard_map/ppermute | solution.py:268
  49.9 2.8 %solve.1.solved_ref = f32[2,32,128]{2,1,0:T(8,128)S(1)} custom-call(f32[64,128]{1,0:T(8,128)S(1)} %add.33.fa_ref, f32[64,128]{1,0:T(8,128)S(1)} %collective-permute-done.8.fb_ref, f32[64,128]{1,0:T(8,128)S(1)} %get-tuple-element.23.grad_ref), custom_call_target="tpu_custom_call" | custom-call | bytes 8000000 | tf_op jit(solution)/shard_map/solve/pallas_call | solution.py:186
  52.7 0.0 collective-permute-done.14
  52.7 0.1 pad_maximum_fusion.q_ref
  52.8 0.8 %contract.1 = f32[2,64]{1,0:T(2,128)S(1)} custom-call(f32[2,32,128]{2,1,0:T(8,128)S(1)} %solve.1.solved_ref, f32[64,32,128]{2,1,0:T(8,128)S(1)} %pad_maximum_fusion.q_ref), custom_call_target="tpu_custom_call" | custom-call | tf_op jit(solution)/shard_map/contract/pallas_call | solution.py:229
  53.6 7.8 %collective-permute-start.15 = (f32[2,64]{1,0:T(2,128)S(1)}, f32[2,64]{1,0:T(2,128)S(1)}, u32[]{:S(2)}, u32[]{:S(2)}) collective-permute-start(f32[2,64]{1,0:T(2,128)S(1)} %contract.1), channel_id=1, source_target_pairs={{0,1},{1,0},{2,3},{3,2},{4,5},{5,4},{6,7},{7,6},{8,9},{9,8},{10,11... | collective-permute-start | bytes 1544 | tf_op jit(solution)/shard_map/ppermute | solution.py:272
  61.4 0.8 %collective-permute-done.15 = f32[2,64]{1,0:T(2,128)S(1)} collective-permute-done((f32[2,64]{1,0:T(2,128)S(1)}, f32[2,64]{1,0:T(2,128)S(1)}, u32[]{:S(2)}, u32[]{:S(2)}) %collective-permute-start.15) | collective-permute-done | bytes 544 | tf_op jit(solution)/shard_map/ppermute | solution.py:272
  62.2 1.6 %collective-permute-start.16 = (f32[2,64]{1,0:T(2,128)S(1)}, f32[2,64]{1,0:T(2,128)S(1)}, u32[]{:S(2)}, u32[]{:S(2)}) collective-permute-start(f32[2,64]{1,0:T(2,128)S(1)} %add.34), channel_id=1, source_target_pairs={{0,2},{1,3},{2,0},{3,1},{4,6},{5,7},{6,4},{7,5},{8,10},{9,11},{10,... | collective-permute-start | bytes 1544 | tf_op jit(solution)/shard_map/ppermute | solution.py:273
  63.8 2.4 %collective-permute-done.16 = f32[2,64]{1,0:T(2,128)S(1)} collective-permute-done((f32[2,64]{1,0:T(2,128)S(1)}, f32[2,64]{1,0:T(2,128)S(1)}, u32[]{:S(2)}, u32[]{:S(2)}) %collective-permute-start.16) | collective-permute-done | bytes 544 | tf_op jit(solution)/shard_map/ppermute | solution.py:273
  66.1 0.6 add.35
  (13 shorter events, 0.2 us)
Async XLA Ops:
  0.0 6.2 %copy-start = (f32[4,1,64,64]{3,2,1,0:T(8,128)S(1)}, f32[4,1,64,64]{3,2,1,0:T(8,128)}, u32[]{:S(2)}) copy-start(f32[4,1,64,64]{3,2,1,0:T(8,128)} %rest_0_.1) | copy-start | bytes 196612
  2.8 6.3 %collective-permute-start = (f32[512,128]{1,0:T(8,128)S(1)}, f32[512,128]{1,0:T(8,128)S(1)}, u32[]{:S(2)}, u32[]{:S(2)}) collective-permute-start(f32[512,128]{1,0:T(8,128)S(1)} %project.4), channel_id=1, source_target_pairs={{0,1},{1,0},{2,3},{3,2},{4,5},{5,4},{6,7},{7,6},{8,9},{9,8},{10,11... | collective-permute-start | bytes 786440 | tf_op jit(solution)/shard_map/ppermute | solution.py:253
  9.1 7.8 %collective-permute-start.9 = (f32[1,32,128]{2,1,0:T(8,128)S(1)}, f32[1,32,128]{2,1,0:T(8,128)S(1)}, u32[]{:S(2)}, u32[]{:S(2)}) collective-permute-start(f32[1,32,128]{2,1,0:T(8,128)S(1)} %get-tuple-element.25), channel_id=1, source_target_pairs={{0,32},{4,36},{8,40},{12,44},{16,48},{20,52},{24,56},{28,60},{32,0... | collective-permute-start | bytes 49160 | tf_op jit(solution)/shard_map/ppermute | solution.py:249
  10.5 14.3 %collective-permute-start.1 = (f32[512,128]{1,0:T(8,128)S(1)}, f32[512,128]{1,0:T(8,128)S(1)}, u32[]{:S(2)}, u32[]{:S(2)}) collective-permute-start(f32[512,128]{1,0:T(8,128)S(1)} %add.27), channel_id=1, source_target_pairs={{0,2},{1,3},{2,0},{3,1},{4,6},{5,7},{6,4},{7,5},{8,10},{9,11},{10,... | collective-permute-start | bytes 786440 | tf_op jit(solution)/shard_map/ppermute | solution.py:256
  16.2 8.6 %collective-permute-start.2 = (f32[512,128]{1,0:T(8,128)S(1)}, f32[512,128]{1,0:T(8,128)S(1)}, u32[]{:S(2)}, u32[]{:S(2)}) collective-permute-start(f32[512,128]{1,0:T(8,128)S(1)} %project.6), channel_id=1, source_target_pairs={{0,1},{1,0},{2,3},{3,2},{4,5},{5,4},{6,7},{7,6},{8,9},{9,8},{10,11... | collective-permute-start | bytes 786440 | tf_op jit(solution)/shard_map/ppermute | solution.py:258
  16.9 4.5 %collective-permute-start.10 = (f32[2,32,128]{2,1,0:T(8,128)S(1)}, f32[2,32,128]{2,1,0:T(8,128)S(1)}, u32[]{:S(2)}, u32[]{:S(2)}) collective-permute-start(f32[2,32,128]{2,1,0:T(8,128)S(1)} %pad_maximum_fusion.5), channel_id=1, source_target_pairs={{0,16},{4,20},{8,24},{12,28},{16,0},{20,4},{24,8},{28,12},{32,48},... | collective-permute-start | bytes 98312 | tf_op jit(solution)/shard_map/ppermute | solution.py:249
  21.4 5.3 %collective-permute-start.11 = (f32[4,32,128]{2,1,0:T(8,128)S(1)}, f32[4,32,128]{2,1,0:T(8,128)S(1)}, u32[]{:S(2)}, u32[]{:S(2)}) collective-permute-start(f32[4,32,128]{2,1,0:T(8,128)S(1)} %pad_maximum_fusion.4), channel_id=1, source_target_pairs={{0,96},{4,100},{8,104},{12,108},{16,112},{20,116},{24,120},{28,124... | collective-permute-start | bytes 196616 | tf_op jit(solution)/shard_map/ppermute | solution.py:249
  25.3 2.9 %collective-permute-start.3 = (f32[64,128]{1,0:T(8,128)S(1)}, f32[64,128]{1,0:T(8,128)S(1)}, u32[]{:S(2)}, u32[]{:S(2)}) collective-permute-start(f32[64,128]{1,0:T(8,128)S(1)} %get-tuple-element.22), channel_id=1, source_target_pairs={{0,4},{4,0},{8,12},{12,8},{16,20},{20,16},{24,28},{28,24},{32,36},... | collective-permute-start | bytes 98312 | tf_op jit(solution)/shard_map/ppermute | solution.py:267
  28.1 4.4 %collective-permute-start.12 = (f32[8,32,128]{2,1,0:T(8,128)S(1)}, f32[8,32,128]{2,1,0:T(8,128)S(1)}, u32[]{:S(2)}, u32[]{:S(2)}) collective-permute-start(f32[8,32,128]{2,1,0:T(8,128)S(1)} %pad_maximum_fusion.3), channel_id=1, source_target_pairs={{0,128},{4,132},{8,136},{12,140},{16,144},{20,148},{24,152},{28,15... | collective-permute-start | bytes 393224 | tf_op jit(solution)/shard_map/ppermute | solution.py:249
  28.5 4.0 %collective-permute-start.4 = (f32[64,128]{1,0:T(8,128)S(1)}, f32[64,128]{1,0:T(8,128)S(1)}, u32[]{:S(2)}, u32[]{:S(2)}) collective-permute-start(f32[64,128]{1,0:T(8,128)S(1)} %add.29), channel_id=1, source_target_pairs={{0,12},{4,8},{8,4},{12,0},{16,28},{20,24},{24,20},{28,16},{32,44},... | collective-permute-start | bytes 98312 | tf_op jit(solution)/shard_map/ppermute | solution.py:267
  32.5 8.8 %collective-permute-start.13 = (f32[16,32,128]{2,1,0:T(8,128)S(1)}, f32[16,32,128]{2,1,0:T(8,128)S(1)}, u32[]{:S(2)}, u32[]{:S(2)}) collective-permute-start(f32[16,32,128]{2,1,0:T(8,128)S(1)} %pad_maximum_fusion.2), channel_id=1, source_target_pairs={{0,4},{4,0},{8,12},{12,8},{16,20},{20,16},{24,28},{28,24},{32,36},... | collective-permute-start | bytes 786440 | tf_op jit(solution)/shard_map/ppermute | solution.py:249
  33.3 2.8 %collective-permute-start.5 = (f32[64,128]{1,0:T(8,128)S(1)}, f32[64,128]{1,0:T(8,128)S(1)}, u32[]{:S(2)}, u32[]{:S(2)}) collective-permute-start(f32[64,128]{1,0:T(8,128)S(1)} %add.30), channel_id=1, source_target_pairs={{0,16},{4,20},{8,24},{12,28},{16,0},{20,4},{24,8},{28,12},{32,48},... | collective-permute-start | bytes 98312 | tf_op jit(solution)/shard_map/ppermute | solution.py:267
  36.0 5.3 %collective-permute-start.6 = (f32[64,128]{1,0:T(8,128)S(1)}, f32[64,128]{1,0:T(8,128)S(1)}, u32[]{:S(2)}, u32[]{:S(2)}) collective-permute-start(f32[64,128]{1,0:T(8,128)S(1)} %add.31), channel_id=1, source_target_pairs={{0,96},{4,100},{8,104},{12,108},{16,112},{20,116},{24,120},{28,124... | collective-permute-start | bytes 98312 | tf_op jit(solution)/shard_map/ppermute | solution.py:267
  41.4 11.3 %collective-permute-start.14 = (f32[32,32,128]{2,1,0:T(8,128)S(1)}, f32[32,32,128]{2,1,0:T(8,128)S(1)}, u32[]{:S(2)}, u32[]{:S(2)}) collective-permute-start(f32[32,32,128]{2,1,0:T(8,128)S(1)} %pad_maximum_fusion.1), channel_id=1, source_target_pairs={{0,12},{4,8},{8,4},{12,0},{16,28},{20,24},{24,20},{28,16},{32,44},... | collective-permute-start | bytes 1572872 | tf_op jit(solution)/shard_map/ppermute | solution.py:249
  43.4 3.7 %collective-permute-start.7 = (f32[64,128]{1,0:T(8,128)S(1)}, f32[64,128]{1,0:T(8,128)S(1)}, u32[]{:S(2)}, u32[]{:S(2)}) collective-permute-start(f32[64,128]{1,0:T(8,128)S(1)} %add.32), channel_id=1, source_target_pairs={{0,32},{4,36},{8,40},{12,44},{16,48},{20,52},{24,56},{28,60},{32,0... | collective-permute-start | bytes 98312 | tf_op jit(solution)/shard_map/ppermute | solution.py:267
  47.1 2.8 %collective-permute-start.8 = (f32[64,128]{1,0:T(8,128)S(1)}, f32[64,128]{1,0:T(8,128)S(1)}, u32[]{:S(2)}, u32[]{:S(2)}) collective-permute-start(f32[64,128]{1,0:T(8,128)S(1)} %add.33.fa_ref), channel_id=1, source_target_pairs={{0,128},{4,132},{8,136},{12,140},{16,144},{20,148},{24,152},{28,15... | collective-permute-start | bytes 98312 | tf_op jit(solution)/shard_map/ppermute | solution.py:268
  53.6 8.6 %collective-permute-start.15 = (f32[2,64]{1,0:T(2,128)S(1)}, f32[2,64]{1,0:T(2,128)S(1)}, u32[]{:S(2)}, u32[]{:S(2)}) collective-permute-start(f32[2,64]{1,0:T(2,128)S(1)} %contract.1), channel_id=1, source_target_pairs={{0,1},{1,0},{2,3},{3,2},{4,5},{5,4},{6,7},{7,6},{8,9},{9,8},{10,11... | collective-permute-start | bytes 1544 | tf_op jit(solution)/shard_map/ppermute | solution.py:272
  62.2 3.9 %collective-permute-start.16 = (f32[2,64]{1,0:T(2,128)S(1)}, f32[2,64]{1,0:T(2,128)S(1)}, u32[]{:S(2)}, u32[]{:S(2)}) collective-permute-start(f32[2,64]{1,0:T(2,128)S(1)} %add.34), channel_id=1, source_target_pairs={{0,2},{1,3},{2,0},{3,1},{4,6},{5,7},{6,4},{7,5},{8,10},{9,11},{10,... | collective-permute-start | bytes 1544 | tf_op jit(solution)/shard_map/ppermute | solution.py:273
